TPU v7x, 128 devices: a whole 4x4x4 slice. The times are simulated.
128 devices in a mesh: row: 8 (over z, y_hi), col: 16 (over x, y_lo, core).
Axes of the slice: x: 4, y: 4 (y_hi: 2, y_lo: 2; y = y_hi * 2 + y_lo), z: 4, core: 2. Of those that a mesh axis runs over, the one named last changes fastest.
Arguments:
- obj: float32 [2, 2048, 4096], P(None, 'row', 'col'), may hold values from -4.2 to 4.2
- probe: float32 [2, 256, 256], replicated, may hold values from -4.2 to 4.2
- amplitudes: bfloat16 [512, 256, 256], P(('row', 'col')), may hold values from 0.049804688 to 4
- positions: int32 [512, 2], replicated, may hold values from 0 to 3840, as said below
Outputs:
- new_object: float32 [2, 2048, 4096], P(None, 'row', 'col')
- new_probe: float32 [2, 256, 256], replicated
Inputs may be any that keep to these rules, and one draw needn't show every extreme that they name: `positions`: entry p is the top-left cell (row, column) of pattern p's window of 256 x 256 cells, which lies inside the object. Pattern p is held by device p // 4 in row-major order of (row, col), and its row offset lies in that device's band of 256 object rows. One device holds at most 2 patterns whose window starts in one tile, and exactly 2 for some tile in every draw; at most 8 windows start in one tile, and in every row of tiles exactly 8 start in one tile.
All inputs are finite; a program needn't handle non-finite values.
Results may differ from a plain program's by a relative error of at most 0.0018.
Values may be sent and summed in bfloat16 or wider, within the bound.
A program may use at most 128 MiB of HBM per device.

v0:
```python
import jax
import jax.numpy as jnp
from jax import lax
from jax.sharding import PartitionSpec as P

ITERS = 2
SEND = 2


amplitude_floor = 0.1
object_regular = 0.5
probe_regular = 1.0
highest = lax.Precision.HIGHEST


def passed_along(value, axis, steps):
    count = lax.axis_size(axis)
    leading, last = (max(0, -steps), min(count, count - steps))
    return lax.ppermute(value, axis, [(source, source + steps) for source in range(leading, last)])


def dft_tables(order):
    counter = jnp.arange(order, dtype=jnp.int32)
    phases = counter[:, None] * counter[None, :] % order
    angles = phases.astype(jnp.float32) * (2.0 * jnp.pi / order)
    norming = 1.0 / jnp.sqrt(jnp.float32(order))
    return (jnp.cos(angles) * norming, -jnp.sin(angles) * norming)


def left_apply(tables, real_part, imag_part):
    first = jnp.einsum("ab,sbc->sac", tables[0], real_part, precision=highest)
    second = jnp.einsum("ab,sbc->sac", tables[1], imag_part, precision=highest)
    third = jnp.einsum("ab,sbc->sac", tables[2], real_part + imag_part, precision=highest)
    return (first - second, third - first - second)


def right_apply(tables, real_part, imag_part):
    first = jnp.einsum("sab,bc->sac", real_part, tables[0], precision=highest)
    second = jnp.einsum("sab,bc->sac", imag_part, tables[1], precision=highest)
    third = jnp.einsum("sab,bc->sac", real_part + imag_part, tables[2], precision=highest)
    return (first - second, third - first - second)


def transform(tables, real_part, imag_part):
    inner_re, inner_im = right_apply(tables, real_part, imag_part)
    return left_apply(tables, inner_re, inner_im)


def extend_tile(current):
    from_right = passed_along(current, "col", -1)
    widened = jnp.concatenate([current, from_right], axis=2)
    from_below = passed_along(widened, "row", -1)
    return jnp.concatenate([widened, from_below], axis=1)


def fold_tile(sums, tile_rows, tile_cols, order):
    from_above = passed_along(sums[:, tile_rows:, :], "row", 1)
    upper = sums[:, :tile_rows, :].at[:, :order, :].add(from_above)
    from_left = passed_along(upper[:, :, tile_cols:], "col", 1)
    return upper[:, :, :tile_cols].at[:, :, :order].add(from_left)


def local(obj, probe, amplitudes, positions):
    col_count = lax.axis_size("col")
    my_row = lax.axis_index("row")
    my_col = lax.axis_index("col")
    device_id = my_row * col_count + my_col
    tile_rows = obj.shape[1]
    tile_cols = obj.shape[2]
    order = probe.shape[1]
    pat_count = amplitudes.shape[0]
    capacity = 2 * pat_count
    slot_count = col_count * SEND
    band_count = col_count * pat_count
    local_index = jnp.arange(pat_count, dtype=jnp.int32)
    my_ids = device_id * pat_count + local_index
    owner_col = positions[my_ids, 1] // tile_cols
    earlier = local_index[None, :] < local_index[:, None]
    same_owner = owner_col[:, None] == owner_col[None, :]
    send_rank = jnp.sum(same_owner & earlier, axis=1)
    send_slot = owner_col * SEND + send_rank
    placing = (jnp.arange(slot_count, dtype=jnp.int32)[:, None] == send_slot[None, :]).astype(
        jnp.bfloat16
    )
    outgoing = jnp.dot(
        placing, amplitudes.reshape(pat_count, order * order), preferred_element_type=jnp.float32
    ).astype(jnp.bfloat16)
    incoming = lax.all_to_all(outgoing, "col", split_axis=0, concat_axis=0, tiled=True)
    band_first = my_row * band_count
    band_pos = lax.dynamic_slice_in_dim(positions, band_first, band_count, 0)
    band_ids = band_first + jnp.arange(band_count, dtype=jnp.int32)
    in_mine = band_pos[:, 1] // tile_cols == my_col
    mine_count = in_mine.astype(jnp.int32)
    band_rank = jnp.cumsum(mine_count) - mine_count
    selection = (band_rank[None, :] == jnp.arange(capacity, dtype=jnp.int32)[:, None]) & in_mine[
        None, :
    ]
    valid = jnp.any(selection, axis=1)
    listed = jnp.sum(jnp.where(selection, band_ids[None, :], 0), axis=1)
    source_dev = listed // pat_count
    source_col = source_dev % col_count
    before = (
        (source_dev[None, :] == source_dev[:, None])
        & (listed[None, :] < listed[:, None])
        & valid[None, :]
    )
    recv_rank = jnp.sum(before, axis=1)
    recv_slot = source_col * SEND + recv_rank
    picking = (
        (jnp.arange(slot_count, dtype=jnp.int32)[None, :] == recv_slot[:, None]) & valid[:, None]
    ).astype(jnp.bfloat16)
    measured = jnp.dot(picking, incoming, preferred_element_type=jnp.float32).reshape(
        capacity, order, order
    )
    spots = positions[listed]
    offset_y = jnp.where(valid, spots[:, 0] - my_row * tile_rows, 0)
    offset_x = jnp.where(valid, spots[:, 1] - my_col * tile_cols, 0)
    weight = valid.astype(jnp.float32)[:, None, None]
    cos_part, sin_part = dft_tables(order)
    forward = (cos_part, sin_part, cos_part + sin_part)
    inverse = (cos_part, -sin_part, cos_part - sin_part)
    current = obj
    probe_now = probe
    for sweep in range(ITERS):
        extended = extend_tile(current)

        def cut_window(top, left):
            return lax.dynamic_slice(extended, (0, top, left), (2, order, order))

        windows = jax.vmap(cut_window)(offset_y, offset_x)
        win_re = windows[:, 0]
        win_im = windows[:, 1]
        probe_re = probe_now[0]
        probe_im = probe_now[1]
        exit_re = probe_re * win_re - probe_im * win_im
        exit_im = probe_re * win_im + probe_im * win_re
        far_re, far_im = transform(forward, exit_re, exit_im)
        factor = measured / jnp.sqrt(far_re * far_re + far_im * far_im + amplitude_floor)
        back_re, back_im = transform(inverse, far_re * factor, far_im * factor)
        change_re = (back_re - exit_re) * weight
        change_im = (back_im - exit_im) * weight
        power = probe_re * probe_re + probe_im * probe_im
        deposits = jnp.stack(
            [
                probe_re * change_re + probe_im * change_im,
                probe_re * change_im - probe_im * change_re,
                power[None] * weight + 0.0 * change_re,
            ],
            axis=1,
        )

        def deposit(index, total):
            start = (0, offset_y[index], offset_x[index])
            block = lax.dynamic_slice(total, start, (3, order, order))
            return lax.dynamic_update_slice(total, block + deposits[index], start)

        sums = lax.fori_loop(
            0, capacity, deposit, jnp.zeros((3, tile_rows + order, tile_cols + order), jnp.float32)
        )
        partials = jnp.stack(
            [
                jnp.sum(win_re * change_re + win_im * change_im, axis=0),
                jnp.sum(win_re * change_im - win_im * change_re, axis=0),
                jnp.sum((win_re * win_re + win_im * win_im) * weight, axis=0),
            ]
        )
        tile_sums = fold_tile(sums, tile_rows, tile_cols, order)
        current = current + tile_sums[:2] / (tile_sums[2] + object_regular)[None]
        totals = lax.psum(partials, ("row", "col"))
        probe_now = probe_now + totals[:2] / (totals[2] + probe_regular)[None]
    return (current, probe_now)


def solution(mesh):
    placed = (P(None, "row", "col"), P(), P(("row", "col"), None, None), P())
    return jax.shard_map(
        local, mesh=mesh, in_specs=placed, out_specs=(P(None, "row", "col"), P()), check_vma=False
    )
```

profile of v0, /device:TPU:1, one launch (start us, length us, event | category | flops | bytes accessed | tf_op | source)
XLA Modules:
  0.0 973.1 jit_solution(13523694036995378047)
XLA Ops:
  16.7 5.9 all_to_all.8
  22.6 5.7 all-to-all-start
  34.0 65.7 %collective-permute-done.1 = f32[2,256,512]{2,1,0:T(8,128)} collective-permute-done((f32[2,256,512]{2,1,0:T(8,128)S(1)}, f32[2,256,512]{2,1,0:T(8,128)}, u32[]{:S(2)}, u32[]{:S(2)}) %collective-permute-start.1) | collective-permute-done | bytes 1048608 | tf_op jit(solution)/shard_map/ppermute | solution.py:19
  103.5 25.5 %while.38 = (s32[]{:T(128)}, f32[2,512,512]{2,1,0:T(8,128)S(1)}, s32[8,3]{0,1:T(4,128)S(1)}, f32[8,2,256,256]{2,3,0,1:T(8,128)}, s32[]{:T(128)}) while((s32[]{:T(128)}, f32[2,512,512]{2,1,0:T(8,128)S(1)}, s32[8,3]{0,1:T(4,128)S(1)}, f32[8,2,256,256]{2,3,0,1:T(8,128)}, s32[]{:T(128)}) %tuple.156), condition=%wide.while_cond.4, body=%wide.while_body.4.sunk | while | flops 2 | bytes 3145853 | solution.py:128
  140.7 5.0 subtract_subtract_fusion.3
  145.7 5.6 fusion.112
  151.3 5.7 fusion.79
  157.0 5.5 all_to_all.10
  169.6 12.4 %fusion.48 = (f32[8,256,256]{1,2,0:T(8,128)S(1)}, f32[8,256,256]{1,2,0:T(8,128)S(1)}) fusion(f32[8,256,256]{1,2,0:T(8,128)} %copy.167, f32[8,256,256]{2,1,0:T(8,128)} %fusion.112, f32[8,256,256]{2,1,0:T(8,128)} %fusion.79, f32[8,256,256]{2,1,0:T(8,128)} %copy-done.9, f32[8,256,256]{2,1,0:T(8,128)} %copy-done.4, f32[8,256,256]{2,1,0:T(8,128)} %copy-done.3), kind=kOutput, calls=%fused_computation.104 | convolution fusion | flops 1618083840 | bytes 16777216 | tf_op jit(solution)/shard_map/ab,sbc->sac/dot_general | solution.py:33
  190.9 4.9 subtract_subtract_fusion.2
  195.8 4.5 fusion.76
  204.8 6.5 fusion.27
  217.5 134.3 %while.36 = (s32[]{:T(128)}, f32[3,512,512]{2,1,0:T(8,128)}, s32[8]{0:T(128)S(1)}, s32[8]{0:T(128)S(1)}, f32[8,3,256,256]{2,3,0,1:T(8,128)}, /*index=5*/s32[]{:T(128)}, s32[]{:T(128)}, s32[]{:T(128)}) while((s32[]{:T(128)}, f32[3,512,512]{2,1,0:T(8,128)}, s32[8]{0:T(128)S(1)}, s32[8]{0:T(128)S(1)}, f32[8,3,256,256]{2,3,0,1:T(8,128)}, ...), condition=%wide.region_6.7_spmd, body=%wide.region_5.6_spmd.sunk | while | flops 196616 | bytes 7078089 | solution.py:157
  225.6 9.0 dynamic_update_slice.16
  242.8 9.1 dynamic_update_slice.16
  259.9 8.6 dynamic_update_slice.16
  276.6 9.4 dynamic_update_slice.16
  294.2 8.3 dynamic_update_slice.16
  310.6 8.3 dynamic_update_slice.16
  327.1 8.3 dynamic_update_slice.16
  343.5 8.3 dynamic_update_slice.16
  353.6 5.0 collective-permute-start.2
  358.5 34.1 %collective-permute-done.2 = f32[3,256,512]{2,1,0:T(8,128)S(1)} collective-permute-done((f32[3,256,512]{2,1,0:T(8,128)S(1)}, f32[3,256,512]{2,1,0:T(8,128)S(1)}, u32[]{:S(2)}, u32[]{:S(2)}) %collective-permute-start.2) | collective-permute-done | bytes 1572896 | tf_op jit(solution)/shard_map/ppermute | solution.py:19
  396.4 8.9 collective-permute-done.3
  408.5 8.3 collective-permute-done.4
  418.5 148.3 %all-reduce.4.cloned.1.call-done = f32[3,256,256]{1,2,0:T(8,128)} async-done(((f32[3,256,256]{1,2,0:T(8,128)}), f32[3,256,256]{1,2,0:T(8,128)}) %all-reduce.4.cloned.1.call-update) | async-done | bytes 786448 | tf_op jit(solution)/shard_map/psum | solution.py:169
  573.7 25.8 %while.39 = (s32[]{:T(128)}, f32[2,512,512]{2,1,0:T(8,128)S(1)}, s32[8,3]{0,1:T(4,128)S(1)}, f32[8,2,256,256]{2,3,0,1:T(8,128)}, s32[]{:T(128)}) while((s32[]{:T(128)}, f32[2,512,512]{2,1,0:T(8,128)S(1)}, s32[8,3]{0,1:T(4,128)S(1)}, f32[8,2,256,256]{2,3,0,1:T(8,128)}, s32[]{:T(128)}) %tuple.172), condition=%wide.while_cond.5, body=%wide.while_body.5.sunk | while | flops 2 | bytes 3145853 | solution.py:128
  602.4 4.5 fusion.110
  611.3 4.9 subtract_subtract_fusion.1
  616.2 4.5 fusion.73
  625.2 5.5 fusion.38
  635.2 4.6 fusion.117
  639.8 4.6 subtract_subtract_fusion
  644.4 4.5 fusion.70
  649.0 4.7 fusion.96
  653.7 6.9 fusion.12
  666.8 133.6 %while.37 = (s32[]{:T(128)}, f32[3,512,512]{2,1,0:T(8,128)}, s32[8]{0:T(128)S(1)}, s32[8]{0:T(128)S(1)}, f32[8,3,256,256]{2,3,0,1:T(8,128)}, /*index=5*/s32[]{:T(128)}, s32[]{:T(128)}, s32[]{:T(128)}) while((s32[]{:T(128)}, f32[3,512,512]{2,1,0:T(8,128)}, s32[8]{0:T(128)S(1)}, s32[8]{0:T(128)S(1)}, f32[8,3,256,256]{2,3,0,1:T(8,128)}, ...), condition=%wide.region_12.13_spmd, body=%wide.region_11.12_spmd.sunk | while | flops 196616 | bytes 7078089 | solution.py:157
  674.9 9.0 dynamic_update_slice.17
  691.9 9.1 dynamic_update_slice.17
  708.9 8.6 dynamic_update_slice.17
  725.5 9.4 dynamic_update_slice.17
  743.0 8.3 dynamic_update_slice.17
  759.3 8.3 dynamic_update_slice.17
  775.7 8.3 dynamic_update_slice.17
  792.0 8.3 dynamic_update_slice.17
  803.2 6.2 collective-permute-start.6
  810.4 32.6 %collective-permute-done.6 = f32[3,256,512]{2,1,0:T(8,128)} collective-permute-done((f32[3,256,512]{2,1,0:T(8,128)}, f32[3,256,512]{2,1,0:T(8,128)}, u32[]{:S(2)}, u32[]{:S(2)}) %collective-permute-start.6) | collective-permute-done | bytes 1572896 | tf_op jit(solution)/shard_map/ppermute | solution.py:19
  849.5 111.2 %all-reduce.6.cloned.1.call-done = f32[3,256,256]{1,2,0:T(8,128)} async-done(((f32[3,256,256]{1,2,0:T(8,128)}), f32[3,256,256]{1,2,0:T(8,128)}) %all-reduce.6.cloned.1.call-update) | async-done | bytes 786448 | tf_op jit(solution)/shard_map/psum | solution.py:169
  (314 shorter events, 230.8 us)
Async XLA Ops:
  7.2 23.1 %collective-permute-start = (f32[2,256,256]{2,1,0:T(8,128)}, f32[2,256,256]{2,1,0:T(8,128)S(1)}, u32[]{:S(2)}, u32[]{:S(2)}) collective-permute-start(f32[2,256,256]{2,1,0:T(8,128)} %param.24), channel_id=1, source_target_pairs={{1,0},{2,1},{3,2},{4,3},{5,4},{6,5},{7,6},{8,7},{9,8},{10,9},{11,1... | collective-permute-start | bytes 1572872 | tf_op jit(solution)/shard_map/ppermute | solution.py:19
  22.6 5.7 copy-start
  22.6 7.4 copy-start.19
  22.6 134.4 %all-to-all-start = ((bf16[16,2,65536]{2,1,0:T(2,128)(2,1)}), bf16[16,2,65536]{2,1,0:T(2,128)(2,1)}, u32[]{:S(2)}, u32[]{:S(2)}) async-start(bf16[16,2,65536]{2,1,0:T(2,128)(2,1)} %all_to_all.8), calls=%async_computation | async-start | bytes 8388608 | tf_op jit(solution)/shard_map/all_to_all | solution.py:88
  28.3 3.6 copy-start.21
  28.3 538.5 %all-reduce.4.cloned.1.call-start = ((), (), s32[]{:S(2)}) async-start(), calls=%async_computation.1 | async-start | bytes 1572864 | tf_op jit(solution)/shard_map/psum | solution.py:169
  30.4 69.3 %collective-permute-start.1 = (f32[2,256,512]{2,1,0:T(8,128)S(1)}, f32[2,256,512]{2,1,0:T(8,128)}, u32[]{:S(2)}, u32[]{:S(2)}) collective-permute-start(f32[2,256,512]{2,1,0:T(8,128)S(1)} %constant_dynamic-update-slice_fusion.2), channel_id=1, source_target_pairs={{16,0},{32,16},{48,32},{64,48},{80,64},{96,80},{112,96},{17,1},{33... | collective-permute-start | bytes 3145736 | tf_op jit(solution)/shard_map/ppermute | solution.py:19
  131.8 8.9 copy-start.1
  136.2 15.1 %copy-start.3 = (f32[8,256,256]{2,1,0:T(8,128)}, f32[8,256,256]{2,1,0:T(8,128)S(1)}, u32[]{:S(2)}) copy-start(f32[8,256,256]{2,1,0:T(8,128)S(1)} %fusion.114) | copy-start | bytes 6291460
  140.7 10.6 %copy-start.4 = (f32[8,256,256]{2,1,0:T(8,128)}, f32[8,256,256]{2,1,0:T(8,128)S(1)}, u32[]{:S(2)}) copy-start(f32[8,256,256]{2,1,0:T(8,128)S(1)} %fusion.126) | copy-start | bytes 6291460
  145.7 5.6 copy-start.9
  195.8 9.0 copy-start.7
  200.3 4.5 copy-start.2
  204.8 6.5 copy-start.18
  204.8 6.5 copy-start.29
  351.9 40.8 %copy-start.6 = (f32[3,512,512]{2,1,0:T(8,128)S(1)}, f32[3,512,512]{2,1,0:T(8,128)}, u32[]{:S(2)}) copy-start(f32[3,512,512]{2,1,0:T(8,128)} %get-tuple-element.270) | copy-start | bytes 9437188
  353.6 39.1 %collective-permute-start.2 = (f32[3,256,512]{2,1,0:T(8,128)S(1)}, f32[3,256,512]{2,1,0:T(8,128)S(1)}, u32[]{:S(2)}, u32[]{:S(2)}) collective-permute-start(f32[3,256,512]{2,1,0:T(8,128)S(1)} %slice.165), channel_id=1, source_target_pairs={{0,16},{16,32},{32,48},{48,64},{64,80},{80,96},{96,112},{1,17},{17... | collective-permute-start | bytes 4718600 | tf_op jit(solution)/shard_map/ppermute | solution.py:19
  393.0 12.5 %copy-start.20 = (f32[2,256,256]{2,1,0:T(8,128)S(1)}, f32[2,256,256]{2,1,0:T(8,128)}, u32[]{:S(2)}) copy-start(f32[2,256,256]{2,1,0:T(8,128)} %param.24) | copy-start | bytes 1572868
  393.1 12.2 %collective-permute-start.3 = (f32[3,256,256]{2,1,0:T(8,128)S(1)}, f32[3,256,256]{2,1,0:T(8,128)S(1)}, u32[]{:S(2)}, u32[]{:S(2)}) collective-permute-start(f32[3,256,256]{2,1,0:T(8,128)S(1)} %slice.219), channel_id=1, source_target_pairs={{0,1},{1,2},{2,3},{3,4},{4,5},{5,6},{6,7},{7,8},{8,9},{9,10},{10,1... | collective-permute-start | bytes 2359304 | tf_op jit(solution)/shard_map/ppermute | solution.py:19
  405.6 164.4 %copy-start.11 = (f32[2,256,256]{2,1,0:T(8,128)}, f32[2,256,256]{2,1,0:T(8,128)S(1)}, u32[]{:S(2)}) copy-start(f32[2,256,256]{2,1,0:T(8,128)S(1)} %fusion.84) | copy-start | bytes 1572868
  405.6 11.2 %collective-permute-start.4 = (f32[2,256,256]{2,1,0:T(8,128)S(1)}, f32[2,256,256]{2,1,0:T(8,128)S(1)}, u32[]{:S(2)}, u32[]{:S(2)}) collective-permute-start(f32[2,256,256]{2,1,0:T(8,128)S(1)} %fusion.84), channel_id=1, source_target_pairs={{1,0},{2,1},{3,2},{4,3},{5,4},{6,5},{7,6},{8,7},{9,8},{10,9},{11,1... | collective-permute-start | bytes 1572872 | tf_op jit(solution)/shard_map/ppermute | solution.py:19
  407.5 10.8 %copy-start.22 = (f32[2,256,256]{2,1,0:T(8,128)S(1)}, f32[2,256,256]{2,1,0:T(8,128)}, u32[]{:S(2)}) copy-start(f32[2,256,256]{2,1,0:T(8,128)} %param.25) | copy-start | bytes 1572868
  408.5 552.2 %all-reduce.6.cloned.1.call-start = ((), (), s32[]{:S(2)}) async-start(), calls=%async_computation.2 | async-start | bytes 1572864 | tf_op jit(solution)/shard_map/psum | solution.py:169
  416.8 1.4 copy-start.23
  417.0 152.9 %collective-permute-start.5 = (f32[2,256,512]{2,1,0:T(8,128)S(1)}, f32[2,256,512]{2,1,0:T(8,128)}, u32[]{:S(2)}, u32[]{:S(2)}) collective-permute-start(f32[2,256,512]{2,1,0:T(8,128)S(1)} %pad_maximum_fusion.4), channel_id=1, source_target_pairs={{16,0},{32,16},{48,32},{64,48},{80,64},{96,80},{112,96},{17,1},{33... | collective-permute-start | bytes 3145736 | tf_op jit(solution)/shard_map/ppermute | solution.py:19
  566.7 3.2 copy-start.24
  568.9 1.0 copy-start.15
  620.7 4.5 copy-start.10
  649.0 4.7 copy-start.8
  653.7 6.9 copy-start.17
  653.7 6.9 copy-start.28
  800.4 9.0 copy-start.25
  800.4 9.0 copy-start.26
  800.4 9.0 copy-start.27
  800.4 42.6 %copy-start.5 = (f32[3,512,512]{2,1,0:T(8,128)S(1)}, f32[3,512,512]{2,1,0:T(8,128)}, u32[]{:S(2)}) copy-start(f32[3,512,512]{2,1,0:T(8,128)} %get-tuple-element.271) | copy-start | bytes 9437188
  803.2 39.8 %collective-permute-start.6 = (f32[3,256,512]{2,1,0:T(8,128)}, f32[3,256,512]{2,1,0:T(8,128)}, u32[]{:S(2)}, u32[]{:S(2)}) collective-permute-start(f32[3,256,512]{2,1,0:T(8,128)} %slice.177), channel_id=1, source_target_pairs={{0,16},{16,32},{32,48},{48,64},{64,80},{80,96},{96,112},{1,17},{17... | collective-permute-start | bytes 4718600 | tf_op jit(solution)/shard_map/ppermute | solution.py:19
  844.8 1.2 copy-start.13
  845.9 115.7 %copy-start.16 = (f32[2,256,256]{1,2,0:T(8,128)S(1)}, f32[2,256,256]{1,2,0:T(8,128)}, u32[]{:S(2)}) copy-start(f32[2,256,256]{1,2,0:T(8,128)} %copy-done.15) | copy-start | bytes 1572868
  846.0 117.8 %copy-start.14 = (f32[3,256,512]{2,1,0:T(8,128)S(1)}, f32[3,256,512]{2,1,0:T(8,128)}, u32[]{:S(2)}) copy-start(f32[3,256,512]{2,1,0:T(8,128)} %copy-done.13) | copy-start | bytes 4718596
  846.0 117.8 %collective-permute-start.7 = (f32[3,256,256]{2,1,0:T(8,128)S(1)}, f32[3,256,256]{2,1,0:T(8,128)}, u32[]{:S(2)}, u32[]{:S(2)}) collective-permute-start(f32[3,256,256]{2,1,0:T(8,128)S(1)} %slice.227), channel_id=1, source_target_pairs={{0,1},{1,2},{2,3},{3,4},{4,5},{5,6},{6,7},{7,8},{8,9},{9,10},{10,1... | collective-permute-start | bytes 2359304 | tf_op jit(solution)/shard_map/ppermute | solution.py:19
  962.8 2.3 copy-start.12
Sparse Core Ops, SparseCore 0:
  408.6 158.0 all-reduce.3
  810.5 150.1 all-reduce.5
where the time goes:
time: 985 us; the launch traced here: 973 us
  waiting for transfers between devices  409 us (42%)
  local copies, waits for them, and re-layouts  268 us (27%)
  matrix products  132 us (13%)
  loops' own time  61.9 us (6%)
  other arithmetic  55.1 us (6%)
  starting transfers between devices  31.4 us (3%)
  between operations  15.1 us (2%)
    psum x2, waiting for transfers between devices, local(): totals = lax.psum(partials, ('row', 'col'))  259 us
    ppermute x8, waiting for transfers between devices, passed_along(): lax.ppermute(value, axis, [(source, source + steps) for source in range(l...  150 us
    dynamic_update_slice x16, local copies, waits for them, and re-layouts, deposit(): return lax.dynamic_update_slice(total, block + deposits[index], start)  139 us
    another operation x2, loops' own time, local(): lax.fori_loop(0, capacity, deposit, jnp.zeros((3, tile_rows + order, tile...  61.4 us
    gather x80, local copies, waits for them, and re-layouts  50.8 us
    dot_general x4, matrix products, left_apply(): jnp.einsum('ab,sbc->sac', tables[2], real_part + imag_part, precision=hig...  31.3 us
    ppermute x8, starting transfers between devices, passed_along(): lax.ppermute(value, axis, [(source, source + steps) for source in range(l...  25.7 us
    add x16, other arithmetic, deposit(): return lax.dynamic_update_slice(total, block + deposits[index], start)  25.4 us
  transfers between devices with their start and end apart: 11, of which 7 were waited for; matrix products, arithmetic and copies ran while one was open for 8% of the time, Pallas kernels for 0%

commit v1 on v0

v1 whole, which is shorter than its diff:
```python
import functools

import jax
import jax.numpy as jnp
import numpy as np
from jax import lax
from jax.experimental import pallas as pl
from jax.experimental.pallas import tpu as pltpu
from jax.sharding import PartitionSpec as P

ITERS = 2
amplitude_floor = 0.1
object_regular = 0.5
probe_regular = 1.0

N = 256
H = 128
STRIP = 32


def real_tables():
    n = np.arange(H)
    out = []
    for odd in (0, 1):
        phase = (n[:, None] * (2 * n[None, :] + odd)) % N
        angle = phase * (2 * np.pi / N)
        re, im = np.cos(angle) / 16.0, -np.sin(angle) / 16.0
        full = np.block([[re, im], [-im, re]]).astype(np.float32)
        out += [full, full.T]
    full = jnp.asarray(np.stack(out))
    high = full.astype(jnp.bfloat16)
    low = (full - high.astype(jnp.float32)).astype(jnp.bfloat16)
    return high, low


def order_tables():
    order = np.concatenate([np.arange(0, N, 2), np.arange(1, N, 2)])
    sel = np.zeros((N, N), np.float32)
    sel[np.arange(N), order] = 1.0
    return jnp.asarray(np.stack([sel, sel.T])).astype(jnp.bfloat16)


def split(x):
    high = x.astype(jnp.bfloat16)
    low = (x - high.astype(jnp.float32)).astype(jnp.bfloat16)
    return high, low


def mm(a, b):
    return jnp.dot(a, b, preferred_element_type=jnp.float32)


def pattern_kernel(
    pos_ref,
    place_ref,
    own_ref,
    right_ref,
    below_ref,
    diag_ref,
    probe_ref,
    amps_ref,
    th_ref,
    tl_ref,
    sel_ref,
    sums_ref,
    part_ref,
    ext,
    raw,
    amp,
    win,
    psi,
    ah,
    al,
    ye,
    yo,
    load_sem,
    amp_sem,
):
    band = place_ref[0]
    my_col = place_ref[1]
    loads = []
    for k, (src, r, c) in enumerate(
        ((own_ref, 0, 0), (right_ref, 0, N), (below_ref, N, 0), (diag_ref, N, N))
    ):
        copy = pltpu.make_async_copy(
            src, ext.at[:, pl.ds(r, N), pl.ds(c, N)], load_sem.at[k]
        )
        copy.start()
        loads.append(copy)
    for r in range(0, 2 * N, STRIP):
        for q in range(2):
            sums_ref[q, pl.ds(r, STRIP), :] = jnp.zeros((STRIP, 2 * N), jnp.float32)
    part_ref[...] = jnp.zeros_like(part_ref)
    for copy in loads:
        copy.wait()

    lane = lax.broadcasted_iota(jnp.int32, (STRIP, H), 1)

    def process(j, top, left):
        fetch = pltpu.make_async_copy(amps_ref.at[j], raw, amp_sem)
        fetch.start()
        r8 = pl.multiple_of((top // 8) * 8, 8)
        dr = top - r8
        c128 = pl.multiple_of((left // H) * H, H)
        dc = left - c128

        def cut(s, _):
            r0 = pl.multiple_of(s * STRIP, STRIP)
            w = []
            for q in range(2):
                block = ext[q, pl.ds(r8 + r0, STRIP + 8), pl.ds(c128, 3 * H)]
                block = pltpu.roll(block, lax.rem(STRIP + 8 - dr, STRIP + 8), 0)[:STRIP]
                turned = [
                    pltpu.roll(block[:, k * H : (k + 1) * H], lax.rem(H - dc, H), 1)
                    for k in range(3)
                ]
                keep = lane < H - dc
                w.append(
                    [
                        jnp.where(keep, turned[0], turned[1]),
                        jnp.where(keep, turned[1], turned[2]),
                    ]
                )
            rows = pl.ds(r0, STRIP)
            x = []
            for k in range(2):
                cols = pl.ds(k * H, H)
                wr, wi = w[0][k], w[1][k]
                win[0, rows, cols] = wr
                win[1, rows, cols] = wi
                pr, pi = probe_ref[0, k, rows, :], probe_ref[1, k, rows, :]
                er = pr * wr - pi * wi
                ei = pr * wi + pi * wr
                psi[0, rows, cols] = er
                psi[1, rows, cols] = ei
                x.append((er, ei))
            for k, z in enumerate(
                (
                    x[0][0] + x[1][0],
                    x[0][1] + x[1][1],
                    x[0][0] - x[1][0],
                    x[0][1] - x[1][1],
                )
            ):
                high, low = split(z)
                ah[k // 2, rows, pl.ds((k % 2) * H, H)] = high
                al[k // 2, rows, pl.ds((k % 2) * H, H)] = low
            return 0

        lax.fori_loop(0, N // STRIP, cut, 0)

        def right_apply(t):
            for k, out in ((0, ye), (1, yo)):
                th, tl = th_ref[2 * k + t], tl_ref[2 * k + t]
                out[...] = mm(ah[k], th) + mm(al[k], th) + mm(ah[k], tl)

        def left_apply(t):
            for k, out in ((0, ye), (1, yo)):
                th, tl = th_ref[2 * k + t], tl_ref[2 * k + t]
                out[...] = mm(th, ah[k]) + mm(th, al[k]) + mm(tl, ah[k])

        def put(k, rows, cols, z):
            high, low = split(z)
            ah[k, rows, cols] = high
            al[k, rows, cols] = low

        right_apply(0)

        def rows_forward(s, _):
            r0 = pl.multiple_of(s * STRIP, STRIP)
            up, down = pl.ds(r0, STRIP), pl.ds(r0 + H, STRIP)
            for k, src in ((0, ye), (1, yo)):
                cols = pl.ds(k * H, H)
                for q in range(2):
                    part = pl.ds(q * H, H)
                    a, b = src[up, part], src[down, part]
                    dest = up if q == 0 else down
                    put(0, dest, cols, a + b)
                    put(1, dest, cols, a - b)
            return 0

        lax.fori_loop(0, H // STRIP, rows_forward, 0)
        left_apply(1)
        fetch.wait()
        amp[...] = mm(mm(sel_ref[0], raw[...]).astype(jnp.bfloat16), sel_ref[1])

        def modulus(s, _):
            r0 = pl.multiple_of(s * STRIP, STRIP)
            up, down = pl.ds(r0, STRIP), pl.ds(r0 + H, STRIP)
            for k, src in ((0, ye), (1, yo)):
                re, im = src[up, :], src[down, :]
                m = amp[pl.ds(r0 + k * H, STRIP), :]
                f = m * lax.rsqrt(re * re + im * im + amplitude_floor)
                put(k, up, slice(None), re * f)
                put(k, down, slice(None), im * f)
            return 0

        lax.fori_loop(0, H // STRIP, modulus, 0)
        left_apply(0)

        def rows_back(s, _):
            r0 = pl.multiple_of(s * STRIP, STRIP)
            up, down = pl.ds(r0, STRIP), pl.ds(r0 + H, STRIP)
            for q, src_rows in ((0, up), (1, down)):
                part = pl.ds(q * H, H)
                e, o = ye[src_rows, :], yo[src_rows, :]
                for dest, z in ((up, e + o), (down, e - o)):
                    put(0, dest, part, z[:, :H])
                    put(1, dest, part, z[:, H:])
            return 0

        lax.fori_loop(0, H // STRIP, rows_back, 0)
        right_apply(1)

        def finish(s, _):
            r0 = pl.multiple_of(s * STRIP, STRIP)
            rows = pl.ds(r0, STRIP)
            e_re, e_im = ye[rows, :H], ye[rows, H:]
            o_re, o_im = yo[rows, :H], yo[rows, H:]
            term = [[], []]
            for k in range(2):
                cols = pl.ds(k * H, H)
                br = e_re + o_re if k == 0 else e_re - o_re
                bi = e_im + o_im if k == 0 else e_im - o_im
                cr = br - psi[0, rows, cols]
                ci = bi - psi[1, rows, cols]
                pr, pi = probe_ref[0, k, rows, :], probe_ref[1, k, rows, :]
                wr, wi = win[0, rows, cols], win[1, rows, cols]
                term[0].append(pr * cr + pi * ci)
                term[1].append(pr * ci - pi * cr)
                part_ref[0, k, rows, :] += wr * cr + wi * ci
                part_ref[1, k, rows, :] += wr * ci - wi * cr
                part_ref[2, k, rows, :] += wr * wr + wi * wi
            for q in range(2):
                deposit(sums_ref.at[q], r8 + r0, c128, dr, dc, lane, term[q])
            return 0

        lax.fori_loop(0, N // STRIP, finish, 0)

    def visit(i, _):
        j = band * 64 + i
        y, x = pos_ref[2 * j], pos_ref[2 * j + 1]

        @pl.when(x // N == my_col)
        def _():
            process(i, y - band * N, x - my_col * N)

        return 0

    lax.fori_loop(0, 64, visit, 0)


def deposit(sums, row, col, dr, dc, lane, halves):
    a, b = (pltpu.roll(z, dc, 1) for z in halves)
    hold = lane < dc
    zero = jnp.zeros_like(a)
    wide = jnp.concatenate(
        [jnp.where(hold, zero, a), jnp.where(hold, a, b), jnp.where(hold, b, zero)],
        axis=1,
    )
    tall = jnp.concatenate([wide, jnp.zeros((8, 3 * H), jnp.float32)], axis=0)
    tall = pltpu.roll(tall, dr, 0)
    spot = (pl.ds(pl.multiple_of(row, 8), STRIP + 8), pl.ds(col, 3 * H))
    sums[spot] = sums[spot] + tall


def weights_kernel(pos_ref, place_ref, probe_ref, out_ref, total):
    band = place_ref[0]
    my_col = place_ref[1]
    lane = lax.broadcasted_iota(jnp.int32, (STRIP, H), 1)
    for r in range(0, 3 * N, STRIP):
        total[pl.ds(r, STRIP), :] = jnp.zeros((STRIP, 3 * N), jnp.float32)

    def visit(j, _):
        y, x = pos_ref[2 * j], pos_ref[2 * j + 1]
        top = y - band * N + N
        left = x - my_col * N + N

        @pl.when((top > 0) & (left > 0) & (top < 2 * N) & (left < 2 * N))
        def _():
            r8 = (top // 8) * 8
            c128 = pl.multiple_of((left // H) * H, H)

            def strip(s, _):
                rows = pl.ds(pl.multiple_of(s * STRIP, STRIP), STRIP)
                halves = []
                for k in range(2):
                    cols = pl.ds(k * H, H)
                    pr, pi = probe_ref[0, k, rows, :], probe_ref[1, k, rows, :]
                    halves.append(pr * pr + pi * pi)
                deposit(
                    total, r8 + s * STRIP, c128, top - r8, left - c128, lane, halves
                )
                return 0

            lax.fori_loop(0, N // STRIP, strip, 0)

        return 0

    first = jnp.maximum(band - 1, 0) * 64
    lax.fori_loop(first, (band + 1) * 64, visit, 0)
    out_ref[...] = total[N : 2 * N, N : 2 * N]


SMEM = pl.BlockSpec(memory_space=pltpu.SMEM)
VMEM = pl.BlockSpec(memory_space=pltpu.VMEM)
ANY = pl.BlockSpec(memory_space=pl.ANY)


def run_patterns(pos, place, tiles, probe, gathered, high, low, sel):
    f32, bf16 = jnp.float32, jnp.bfloat16
    return pl.pallas_call(
        pattern_kernel,
        out_shape=(
            jax.ShapeDtypeStruct((2, 2 * N, 2 * N), f32),
            jax.ShapeDtypeStruct((3, 2, N, H), f32),
        ),
        in_specs=[SMEM, SMEM, ANY, ANY, ANY, ANY, VMEM, ANY, VMEM, VMEM, VMEM],
        out_specs=(VMEM, VMEM),
        scratch_shapes=[
            pltpu.VMEM((2, 2 * N, 2 * N), f32),
            pltpu.VMEM((N, N), bf16),
            pltpu.VMEM((N, N), f32),
            pltpu.VMEM((2, N, N), f32),
            pltpu.VMEM((2, N, N), f32),
            pltpu.VMEM((2, N, N), bf16),
            pltpu.VMEM((2, N, N), bf16),
            pltpu.VMEM((N, N), f32),
            pltpu.VMEM((N, N), f32),
            pltpu.SemaphoreType.DMA((4,)),
            pltpu.SemaphoreType.DMA,
        ],
        compiler_params=pltpu.CompilerParams(vmem_limit_bytes=40 * 2**20),
        name="patterns",
    )(pos, place, *tiles, probe, gathered, high, low, sel)


def run_weights(pos, place, probe):
    return pl.pallas_call(
        weights_kernel,
        out_shape=jax.ShapeDtypeStruct((N, N), jnp.float32),
        in_specs=[SMEM, SMEM, VMEM],
        out_specs=VMEM,
        scratch_shapes=[pltpu.VMEM((3 * N, 3 * N), jnp.float32)],
        compiler_params=pltpu.CompilerParams(vmem_limit_bytes=16 * 2**20),
        name="weights",
    )(pos, place, probe)


MESH = pl.DeviceIdType.MESH


def probe_kernel(
    part_ref,
    old_ref,
    out_ref,
    pair,
    half,
    from_x,
    quarter,
    from_y,
    small,
    from_z,
    send_sem,
    recv_sem,
):
    row, col = lax.axis_index("row"), lax.axis_index("col")
    z, y_hi = row // 2, row % 2
    x, y_lo, core = col // 4, (col // 2) % 2, col % 2
    y = y_hi * 2 + y_lo

    def device(z, y, x, core):
        return (z * 2 + y // 2, x * 4 + (y % 2) * 2 + core)

    twin = device(z, y, x, 1 - core)
    on_x = [device(z, y, (x + d) % 4, core) for d in (1, 2, 3)]
    on_y = [device(z, (y + d) % 4, x, core) for d in (1, 2, 3)]
    on_z = [device((z + d) % 4, y, x, core) for d in (1, 2, 3)]
    barrier = pltpu.get_barrier_semaphore()
    for peer in (twin, *on_x, *on_y, *on_z):
        pl.semaphore_signal(barrier, inc=1, device_id=peer, device_id_type=MESH)
    pl.semaphore_wait(barrier, 10)

    count = [0]

    def send(src, dst, peer):
        k = count[0]
        count[0] += 1
        copy = pltpu.make_async_remote_copy(
            src_ref=src,
            dst_ref=dst,
            send_sem=send_sem.at[k],
            recv_sem=recv_sem.at[k],
            device_id=peer,
            device_id_type=MESH,
        )
        copy.start()
        return copy

    def finish(copies):
        for copy in copies:
            copy.wait()

    finish([send(part_ref.at[:, 1 - core], pair, twin)])
    for q in range(3):
        half[q] = part_ref[q, core] + pair[q]
    finish(
        [
            send(
                half.at[:, pl.ds(pl.multiple_of((x + d) % 4 * 64, 64), 64), :],
                from_x.at[d - 1],
                on_x[d - 1],
            )
            for d in (1, 2, 3)
        ]
    )
    mine = pl.ds(pl.multiple_of(x * 64, 64), 64)
    quarter[...] = (half[:, mine, :] + from_x[0]) + (from_x[1] + from_x[2])
    finish(
        [
            send(
                quarter.at[:, pl.ds(pl.multiple_of((y + d) % 4 * 16, 16), 16), :],
                from_y.at[d - 1],
                on_y[d - 1],
            )
            for d in (1, 2, 3)
        ]
    )
    mine = pl.ds(pl.multiple_of(y * 16, 16), 16)
    small[...] = (quarter[:, mine, :] + from_y[0]) + (from_y[1] + from_y[2])
    copies = [send(small, from_z.at[z], peer) for peer in on_z]
    from_z[z] = small[...]
    finish(copies)
    total = (from_z[0] + from_z[1]) + (from_z[2] + from_z[3])
    rows = pl.ds(pl.multiple_of(x * 64 + y * 16, 16), 16)
    for q in range(2):
        out_ref[q, core, rows, :] = old_ref[q, core, rows, :] + total[q] / (
            total[2] + probe_regular
        )
    piece = out_ref.at[:, core, rows, :]
    finish([send(piece, piece, peer) for peer in on_y])
    piece = out_ref.at[:, core, pl.ds(pl.multiple_of(x * 64, 64), 64), :]
    finish([send(piece, piece, peer) for peer in on_x])
    piece = out_ref.at[:, core]
    finish([send(piece, piece, twin)])


def run_probe(partials, probe):
    f32 = jnp.float32
    return pl.pallas_call(
        probe_kernel,
        out_shape=jax.ShapeDtypeStruct((2, 2, N, H), f32),
        in_specs=[VMEM, VMEM],
        out_specs=VMEM,
        scratch_shapes=[
            pltpu.VMEM((3, N, H), f32),
            pltpu.VMEM((3, N, H), f32),
            pltpu.VMEM((3, 3, 64, H), f32),
            pltpu.VMEM((3, 64, H), f32),
            pltpu.VMEM((3, 3, 16, H), f32),
            pltpu.VMEM((3, 16, H), f32),
            pltpu.VMEM((4, 3, 16, H), f32),
            pltpu.SemaphoreType.DMA((17,)),
            pltpu.SemaphoreType.DMA((17,)),
        ],
        compiler_params=pltpu.CompilerParams(
            collective_id=1, has_side_effects=True, vmem_limit_bytes=16 * 2**20
        ),
        name="probe_sum",
    )(partials, probe)


def shifts(rows, cols, down):
    near = [(r, r + 1) for r in range(rows - 1)]
    side = [(c, c + 1) for c in range(cols - 1)]
    both = [
        (r * cols + c, (r + 1) * cols + c + 1)
        for r in range(rows - 1)
        for c in range(cols - 1)
    ]
    if not down:
        near, side, both = ([(b, a) for a, b in z] for z in (near, side, both))
    return near, side, both


def neighbours(tile, rows, cols):
    near, side, both = shifts(rows, cols, False)
    return (
        tile,
        lax.ppermute(tile, "col", side),
        lax.ppermute(tile, "row", near),
        lax.ppermute(tile, ("row", "col"), both),
    )


def local(rows, cols, obj, probe, amplitudes, positions):
    place = jnp.stack([lax.axis_index("row"), lax.axis_index("col")]).astype(jnp.int32)
    pos = positions.reshape(-1)
    high, low = real_tables()
    sel = order_tables()
    gathered = lax.all_gather(amplitudes, "col", tiled=True)
    near, side, both = shifts(rows, cols, True)
    tile = obj
    illum = jnp.stack([probe[:, :, :H], probe[:, :, H:]], axis=1)
    for sweep in range(ITERS):
        tiles = neighbours(tile, rows, cols)
        sums, partials = run_patterns(pos, place, tiles, illum, gathered, high, low, sel)
        from_left = lax.ppermute(sums[:, :N, N:], "col", side)
        from_above = lax.ppermute(sums[:, N:, :N], "row", near)
        from_both = lax.ppermute(sums[:, N:, N:], ("row", "col"), both)
        weights = run_weights(pos, place, illum)
        grad = sums[:, :N, :N] + from_left + from_above + from_both
        tile = tile + grad / (weights + object_regular)[None]
        illum = run_probe(partials, illum)
    return tile, jnp.concatenate([illum[:, 0], illum[:, 1]], axis=2)


def solution(mesh):
    rows, cols = mesh.shape["row"], mesh.shape["col"]
    placed = (P(None, "row", "col"), P(), P(("row", "col"), None, None), P())
    return jax.shard_map(
        functools.partial(local, rows, cols),
        mesh=mesh,
        in_specs=placed,
        out_specs=(P(None, "row", "col"), P()),
        check_vma=False,
    )
```

time: 985 us -> 311 us (0.32); the launches traced: 973 us -> 311 us
  waiting for transfers between devices: 409 us -> 63.9 us
  local copies, waits for them, and re-layouts: 268 us -> 2.41 us
  Pallas kernels: 0 us -> 145 us
  matrix products: 132 us -> 0 us
  loops' own time: 61.9 us -> 0 us
  other arithmetic: 55.1 us -> 2.21 us
  starting transfers between devices: 31.4 us -> 82.6 us
    psum x2 -> x0, waiting for transfers between devices: 259 us -> none  [local(): totals = lax.psum(partials, ('row', 'col'))]
    pallas_call x0 -> x6, Pallas kernels: none -> 145 us  [the longest x2 91.3 us: run_probe(): pl.pallas_call(probe_kernel, out_shape=jax.ShapeDtypeStruct((2, 2, N, H),...]
    dynamic_update_slice x16 -> x0, local copies, waits for them, and re-layouts: 139 us -> none  [deposit(): return lax.dynamic_update_slice(total, block + deposits[index], start)]
    dot_general x26 -> x0, matrix products: 132 us -> none  [the longest x4 31.3 us: left_apply(): jnp.einsum('ab,sbc->sac', tables[2], real_part + imag_part, precision=hig...]
    ppermute x8 -> x12, waiting for transfers between devices: 150 us -> 45.8 us  [the longest x2 18.1 us: neighbours(): lax.ppermute(tile, ('row', 'col'), both)]
    another operation x4 -> x0, loops' own time: 61.9 us -> none  [the longest x2 61.4 us: local(): lax.fori_loop(0, capacity, deposit, jnp.zeros((3, tile_rows + order, tile...]
    ppermute x8 -> x12, starting transfers between devices: 25.7 us -> 82.6 us  [the longest x2 64.1 us: local(): from_both = lax.ppermute(sums[:, N:, N:], ('row', 'col'), both)]
    gather x82 -> x0, local copies, waits for them, and re-layouts: 52.7 us -> none
  transfers between devices with their start and end apart: 11 -> 13, of which waited for: 7 -> 4; matrix products, arithmetic and copies ran while one was open for 8% -> 1% of each run, Pallas kernels for 0% -> 34%
where the time goes in v1:
time: 311 us
  Pallas kernels  145 us (47%)
  starting transfers between devices  82.6 us (27%)
  waiting for transfers between devices  63.9 us (21%)
  between operations  14.3 us (5%)
    pallas_call x2, Pallas kernels, run_probe(): pl.pallas_call(probe_kernel, out_shape=jax.ShapeDtypeStruct((2, 2, N, H),...  91.3 us
    ppermute x2, starting transfers between devices, local(): from_both = lax.ppermute(sums[:, N:, N:], ('row', 'col'), both)  64.1 us
    pallas_call x2, Pallas kernels, run_patterns(): pl.pallas_call(pattern_kernel, out_shape=(jax.ShapeDtypeStruct((2, 2 * N,...  38.3 us
    ppermute x2, waiting for transfers between devices, neighbours(): lax.ppermute(tile, ('row', 'col'), both)  18.1 us
    all_gather x1, waiting for transfers between devices, local(): gathered = lax.all_gather(amplitudes, 'col', tiled=True)  17.5 us
    pallas_call x2, Pallas kernels, run_weights(): pl.pallas_call(weights_kernel, out_shape=jax.ShapeDtypeStruct((N, N), jnp...  15.5 us
    ppermute x2, waiting for transfers between devices, neighbours(): lax.ppermute(tile, 'row', near)  13.8 us
    ppermute x2, waiting for transfers between devices, local(): from_both = lax.ppermute(sums[:, N:, N:], ('row', 'col'), both)  13.8 us
  transfers between devices with their start and end apart: 13, of which 4 were waited for; matrix products, arithmetic and copies ran while one was open for 1% of the time, Pallas kernels for 34%

profile of v1, /device:TPU:1, one launch (start us, length us, event | category | flops | bytes accessed | tf_op | source)
XLA Modules:
  0.0 310.6 jit_solution(3194397569330030406)
XLA Ops:
  7.2 0.0 copy-start.3
  7.2 0.0 copy-start
  7.2 0.0 copy-start.1
  7.2 0.0 copy-start.2
  7.2 0.0 all-gather.2.cloned.1.call-start
  7.3 0.7 all-gather.2.cloned.1.call-update
  7.9 1.3 collective-permute-start.2
  9.2 1.3 collective-permute-start.1
  10.5 3.3 %collective-permute-start = (f32[2,256,256]{2,1,0:T(8,128)}, f32[2,256,256]{2,1,0:T(8,128)}, u32[]{:S(2)}, u32[]{:S(2)}) collective-permute-start(f32[2,256,256]{2,1,0:T(8,128)} %own_ref.1), channel_id=1, source_target_pairs={{1,0},{2,1},{3,2},{4,3},{5,4},{6,5},{7,6},{8,7},{9,8},{10,9},{11,1... | collective-permute-start | bytes 1572872 | tf_op jit(solution)/shard_map/ppermute | solution.py:490
  13.9 0.8 copy.11
  14.7 0.2 reshape.9.pos_ref
  14.9 0.1 pad_add_fusion.place_ref
  15.0 1.1 slice_bitcast_fusion.3
  16.1 18.1 %collective-permute-done.2.diag_ref = f32[2,256,256]{2,1,0:T(8,128)S(1)} collective-permute-done((f32[2,256,256]{2,1,0:T(8,128)}, f32[2,256,256]{2,1,0:T(8,128)S(1)}, u32[]{:S(2)}, u32[]{:S(2)}) %collective-permute-start.2) | collective-permute-done | bytes 524320 | tf_op jit(solution)/shard_map/ppermute | solution.py:492
  34.2 13.8 %collective-permute-done.1.below_ref = f32[2,256,256]{2,1,0:T(8,128)S(1)} collective-permute-done((f32[2,256,256]{2,1,0:T(8,128)}, f32[2,256,256]{2,1,0:T(8,128)S(1)}, u32[]{:S(2)}, u32[]{:S(2)}) %collective-permute-start.1) | collective-permute-done | bytes 524320 | tf_op jit(solution)/shard_map/ppermute | solution.py:491
  48.0 0.0 collective-permute-done.right_ref
  48.0 17.5 %all-gather.2.cloned.1.call-done.amps_ref = bf16[64,256,256]{2,1,0:T(8,128)(2,1)} async-done(((bf16[4,256,256]{2,1,0:T(8,128)(2,1)}), bf16[64,256,256]{2,1,0:T(8,128)(2,1)}) %all-gather.2.cloned.1.call-update) | async-done | bytes 8388624 | tf_op jit(solution)/shard_map/all_gather | solution.py:501
  65.5 0.0 copy-done.3
  65.5 0.0 copy-done
  65.5 19.4 %patterns.2 = (f32[2,512,512]{2,1,0:T(8,128)S(1)}, f32[3,2,256,128]{3,2,1,0:T(8,128)S(1)}) custom-call(s32[1024]{0:T(1024)S(1)} %reshape.9.pos_ref, s32[2]{0:T(128)S(1)} %pad_add_fusion.place_ref, f32[2,256,256]{2,1,0:T(8,128)S(1)} %copy-done.2, f32[2,256,256]{2,1,0:T(8,128)} %collective-permute-done.right_ref, ...), custom_call_target="tpu_custom_call" | custom-call | tf_op jit(solution)/shard_map/patterns/pallas_call | solution.py:312
  84.9 0.1 fusion.1
  85.1 3.3 %collective-permute-start.3 = (f32[2,256,256]{2,1,0:T(8,128)S(1)}, f32[2,256,256]{2,1,0:T(8,128)S(1)}, u32[]{:S(2)}, u32[]{:S(2)}) collective-permute-start(f32[2,256,256]{2,1,0:T(8,128)S(1)} %get-tuple-element.13), channel_id=1, source_target_pairs={{0,1},{1,2},{2,3},{3,4},{4,5},{5,6},{6,7},{7,8},{8,9},{9,10},{10,1... | collective-permute-start | bytes 1572872 | tf_op jit(solution)/shard_map/ppermute | solution.py:508
  88.4 35.2 %collective-permute-start.5 = (f32[2,256,256]{2,1,0:T(8,128)S(1)}, f32[2,256,256]{2,1,0:T(8,128)S(1)}, u32[]{:S(2)}, u32[]{:S(2)}) collective-permute-start(f32[2,256,256]{2,1,0:T(8,128)S(1)} %get-tuple-element.14), channel_id=1, source_target_pairs={{0,17},{1,18},{2,19},{3,20},{4,21},{5,22},{6,23},{7,24},{8,25},{9,... | collective-permute-start | bytes 1572872 | tf_op jit(solution)/shard_map/ppermute | solution.py:510
  123.6 1.3 collective-permute-start.4
  124.9 7.7 %weights.2 = f32[256,256]{1,0:T(8,128)S(1)} custom-call(s32[1024]{0:T(1024)S(1)} %reshape.9.pos_ref, s32[2]{0:T(128)S(1)} %pad_add_fusion.place_ref, f32[2,2,256,128]{3,2,1,0:T(8,128)S(1)} %pad_maximum_fusion.probe_ref.old_ref), custom_call_target="tpu_custom_call" | custom-call | tf_op jit(solution)/shard_map/weights/pallas_call | solution.py:339
  132.7 0.0 collective-permute-done.3
  132.7 13.8 %collective-permute-done.5 = f32[2,256,256]{2,1,0:T(8,128)S(1)} collective-permute-done((f32[2,256,256]{2,1,0:T(8,128)S(1)}, f32[2,256,256]{2,1,0:T(8,128)S(1)}, u32[]{:S(2)}, u32[]{:S(2)}) %collective-permute-start.5) | collective-permute-done | bytes 524320 | tf_op jit(solution)/shard_map/ppermute | solution.py:510
  146.5 0.0 collective-permute-done.4
  146.5 0.2 divide_add_fusion.1.own_ref
  146.7 1.3 collective-permute-start.8
  148.0 1.3 collective-permute-start.7
  149.3 1.9 collective-permute-start.6
  151.3 55.0 %probe_sum.2.probe_ref.old_ref = f32[2,2,256,128]{3,2,1,0:T(8,128)S(1)} custom-call(f32[3,2,256,128]{3,2,1,0:T(8,128)S(1)} %get-tuple-element.7.part_ref, f32[2,2,256,128]{3,2,1,0:T(8,128)S(1)} %pad_maximum_fusion.probe_ref.old_ref), custom_call_target="tpu_custom_call" | custom-call | tf_op jit(solution)/shard_map/probe_sum/pallas_call | solution.py:450
  206.3 7.7 %weights.3 = f32[256,256]{1,0:T(8,128)S(1)} custom-call(s32[1024]{0:T(1024)S(1)} %reshape.9.pos_ref, s32[2]{0:T(128)S(1)} %pad_add_fusion.place_ref, f32[2,2,256,128]{3,2,1,0:T(8,128)S(1)} %probe_sum.2.probe_ref.old_ref), custom_call_target="tpu_custom_call" | custom-call | tf_op jit(solution)/shard_map/weights/pallas_call | solution.py:339
  214.0 0.0 collective-permute-done.8.diag_ref
  214.0 0.0 collective-permute-done.7.below_ref
  214.0 0.0 collective-permute-done.6.right_ref
  214.0 19.0 %patterns.3 = (f32[2,512,512]{2,1,0:T(8,128)S(1)}, f32[3,2,256,128]{3,2,1,0:T(8,128)S(1)}) custom-call(s32[1024]{0:T(1024)S(1)} %reshape.9.pos_ref, s32[2]{0:T(128)S(1)} %pad_add_fusion.place_ref, f32[2,256,256]{2,1,0:T(8,128)S(1)} %divide_add_fusion.1.own_ref, f32[2,256,256]{2,1,0:T(8,128)S(1)} %collective-permute-done.6.right_ref, ...), custom_call_target="tpu_custom_call" | custom-call | tf_op jit(solution)/shard_map/patterns/pallas_call | solution.py:312
  233.0 0.1 fusion
  233.2 2.1 collective-permute-start.9
  235.3 28.9 %collective-permute-start.11 = (f32[2,256,256]{2,1,0:T(8,128)S(1)}, f32[2,256,256]{2,1,0:T(8,128)S(1)}, u32[]{:S(2)}, u32[]{:S(2)}) collective-permute-start(f32[2,256,256]{2,1,0:T(8,128)S(1)} %get-tuple-element.11), channel_id=1, source_target_pairs={{0,17},{1,18},{2,19},{3,20},{4,21},{5,22},{6,23},{7,24},{8,25},{9,... | collective-permute-start | bytes 1572872 | tf_op jit(solution)/shard_map/ppermute | solution.py:510
  264.2 1.3 collective-permute-start.10
  265.5 36.3 %probe_sum.3 = f32[2,2,256,128]{3,2,1,0:T(8,128)S(1)} custom-call(f32[3,2,256,128]{3,2,1,0:T(8,128)S(1)} %get-tuple-element.9.part_ref, f32[2,2,256,128]{3,2,1,0:T(8,128)S(1)} %probe_sum.2.probe_ref.old_ref), custom_call_target="tpu_custom_call" | custom-call | tf_op jit(solution)/shard_map/probe_sum/pallas_call | solution.py:450
  301.9 0.8 pad_maximum_fusion.1
  302.7 0.0 collective-permute-done.9
  302.7 0.0 collective-permute-done.11
  302.7 0.0 collective-permute-done.10
  302.7 1.0 divide_add_fusion
  (6 shorter events, 0.1 us)
Async XLA Ops:
  7.2 58.3 %copy-start.3 = (bf16[2,256,256]{2,1,0:T(8,128)(2,1)S(1)}, bf16[2,256,256]{2,1,0:T(8,128)(2,1)}, u32[]{:S(2)}) copy-start(bf16[2,256,256]{2,1,0:T(8,128)(2,1)} %constant.22.sel_ref) | copy-start | bytes 786436
  7.2 58.3 %copy-start = (bf16[4,256,256]{2,1,0:T(8,128)(2,1)S(1)}, bf16[4,256,256]{2,1,0:T(8,128)(2,1)}, u32[]{:S(2)}) copy-start(bf16[4,256,256]{2,1,0:T(8,128)(2,1)} %constant.21.tl_ref) | copy-start | bytes 1572868
  7.2 58.3 %copy-start.1 = (bf16[4,256,256]{2,1,0:T(8,128)(2,1)S(1)}, bf16[4,256,256]{2,1,0:T(8,128)(2,1)}, u32[]{:S(2)}) copy-start(bf16[4,256,256]{2,1,0:T(8,128)(2,1)} %constant.18.th_ref) | copy-start | bytes 1572868
  7.2 58.3 %copy-start.2 = (f32[2,256,256]{2,1,0:T(8,128)S(1)}, f32[2,256,256]{2,1,0:T(8,128)}, u32[]{:S(2)}) copy-start(f32[2,256,256]{2,1,0:T(8,128)} %own_ref.1) | copy-start | bytes 1572868
  7.2 58.3 %all-gather.2.cloned.1.call-start = ((), (), s32[]{:S(2)}) async-start(), calls=%async_computation | async-start | bytes 8912896 | tf_op jit(solution)/shard_map/all_gather | solution.py:501
  7.9 26.3 %collective-permute-start.2 = (f32[2,256,256]{2,1,0:T(8,128)}, f32[2,256,256]{2,1,0:T(8,128)S(1)}, u32[]{:S(2)}, u32[]{:S(2)}) collective-permute-start(f32[2,256,256]{2,1,0:T(8,128)} %own_ref.1), channel_id=1, source_target_pairs={{17,0},{18,1},{19,2},{20,3},{21,4},{22,5},{23,6},{24,7},{25,8},{26... | collective-permute-start | bytes 1572872 | tf_op jit(solution)/shard_map/ppermute | solution.py:492
  9.2 38.8 %collective-permute-start.1 = (f32[2,256,256]{2,1,0:T(8,128)}, f32[2,256,256]{2,1,0:T(8,128)S(1)}, u32[]{:S(2)}, u32[]{:S(2)}) collective-permute-start(f32[2,256,256]{2,1,0:T(8,128)} %own_ref.1), channel_id=1, source_target_pairs={{16,0},{32,16},{48,32},{64,48},{80,64},{96,80},{112,96},{17,1},{33... | collective-permute-start | bytes 1572872 | tf_op jit(solution)/shard_map/ppermute | solution.py:491
  10.5 37.5 %collective-permute-start = (f32[2,256,256]{2,1,0:T(8,128)}, f32[2,256,256]{2,1,0:T(8,128)}, u32[]{:S(2)}, u32[]{:S(2)}) collective-permute-start(f32[2,256,256]{2,1,0:T(8,128)} %own_ref.1), channel_id=1, source_target_pairs={{1,0},{2,1},{3,2},{4,3},{5,4},{6,5},{7,6},{8,7},{9,8},{10,9},{11,1... | collective-permute-start | bytes 1572872 | tf_op jit(solution)/shard_map/ppermute | solution.py:490
  85.1 47.6 %collective-permute-start.3 = (f32[2,256,256]{2,1,0:T(8,128)S(1)}, f32[2,256,256]{2,1,0:T(8,128)S(1)}, u32[]{:S(2)}, u32[]{:S(2)}) collective-permute-start(f32[2,256,256]{2,1,0:T(8,128)S(1)} %get-tuple-element.13), channel_id=1, source_target_pairs={{0,1},{1,2},{2,3},{3,4},{4,5},{5,6},{6,7},{7,8},{8,9},{9,10},{10,1... | collective-permute-start | bytes 1572872 | tf_op jit(solution)/shard_map/ppermute | solution.py:508
  88.4 58.1 %collective-permute-start.5 = (f32[2,256,256]{2,1,0:T(8,128)S(1)}, f32[2,256,256]{2,1,0:T(8,128)S(1)}, u32[]{:S(2)}, u32[]{:S(2)}) collective-permute-start(f32[2,256,256]{2,1,0:T(8,128)S(1)} %get-tuple-element.14), channel_id=1, source_target_pairs={{0,17},{1,18},{2,19},{3,20},{4,21},{5,22},{6,23},{7,24},{8,25},{9,... | collective-permute-start | bytes 1572872 | tf_op jit(solution)/shard_map/ppermute | solution.py:510
  123.6 22.9 %collective-permute-start.4 = (f32[2,256,256]{2,1,0:T(8,128)S(1)}, f32[2,256,256]{2,1,0:T(8,128)S(1)}, u32[]{:S(2)}, u32[]{:S(2)}) collective-permute-start(f32[2,256,256]{2,1,0:T(8,128)S(1)} %get-tuple-element.15), channel_id=1, source_target_pairs={{0,16},{16,32},{32,48},{48,64},{64,80},{80,96},{96,112},{1,17},{17... | collective-permute-start | bytes 1572872 | tf_op jit(solution)/shard_map/ppermute | solution.py:509
  146.7 67.3 %collective-permute-start.8 = (f32[2,256,256]{2,1,0:T(8,128)S(1)}, f32[2,256,256]{2,1,0:T(8,128)S(1)}, u32[]{:S(2)}, u32[]{:S(2)}) collective-permute-start(f32[2,256,256]{2,1,0:T(8,128)S(1)} %divide_add_fusion.1.own_ref), channel_id=1, source_target_pairs={{17,0},{18,1},{19,2},{20,3},{21,4},{22,5},{23,6},{24,7},{25,8},{26... | collective-permute-start | bytes 1572872 | tf_op jit(solution)/shard_map/ppermute | solution.py:492
  148.0 66.0 %collective-permute-start.7 = (f32[2,256,256]{2,1,0:T(8,128)S(1)}, f32[2,256,256]{2,1,0:T(8,128)S(1)}, u32[]{:S(2)}, u32[]{:S(2)}) collective-permute-start(f32[2,256,256]{2,1,0:T(8,128)S(1)} %divide_add_fusion.1.own_ref), channel_id=1, source_target_pairs={{16,0},{32,16},{48,32},{64,48},{80,64},{96,80},{112,96},{17,1},{33... | collective-permute-start | bytes 1572872 | tf_op jit(solution)/shard_map/ppermute | solution.py:491
  149.3 64.7 %collective-permute-start.6 = (f32[2,256,256]{2,1,0:T(8,128)S(1)}, f32[2,256,256]{2,1,0:T(8,128)S(1)}, u32[]{:S(2)}, u32[]{:S(2)}) collective-permute-start(f32[2,256,256]{2,1,0:T(8,128)S(1)} %divide_add_fusion.1.own_ref), channel_id=1, source_target_pairs={{1,0},{2,1},{3,2},{4,3},{5,4},{6,5},{7,6},{8,7},{9,8},{10,9},{11,1... | collective-permute-start | bytes 1572872 | tf_op jit(solution)/shard_map/ppermute | solution.py:490
  233.2 69.6 %collective-permute-start.9 = (f32[2,256,256]{2,1,0:T(8,128)S(1)}, f32[2,256,256]{2,1,0:T(8,128)S(1)}, u32[]{:S(2)}, u32[]{:S(2)}) collective-permute-start(f32[2,256,256]{2,1,0:T(8,128)S(1)} %get-tuple-element.10), channel_id=1, source_target_pairs={{0,1},{1,2},{2,3},{3,4},{4,5},{5,6},{6,7},{7,8},{8,9},{9,10},{10,1... | collective-permute-start | bytes 1572872 | tf_op jit(solution)/shard_map/ppermute | solution.py:508
  235.3 67.5 %collective-permute-start.11 = (f32[2,256,256]{2,1,0:T(8,128)S(1)}, f32[2,256,256]{2,1,0:T(8,128)S(1)}, u32[]{:S(2)}, u32[]{:S(2)}) collective-permute-start(f32[2,256,256]{2,1,0:T(8,128)S(1)} %get-tuple-element.11), channel_id=1, source_target_pairs={{0,17},{1,18},{2,19},{3,20},{4,21},{5,22},{6,23},{7,24},{8,25},{9,... | collective-permute-start | bytes 1572872 | tf_op jit(solution)/shard_map/ppermute | solution.py:510
  264.2 38.6 %collective-permute-start.10 = (f32[2,256,256]{2,1,0:T(8,128)S(1)}, f32[2,256,256]{2,1,0:T(8,128)S(1)}, u32[]{:S(2)}, u32[]{:S(2)}) collective-permute-start(f32[2,256,256]{2,1,0:T(8,128)S(1)} %get-tuple-element.12), channel_id=1, source_target_pairs={{0,16},{16,32},{32,48},{48,64},{64,80},{80,96},{96,112},{1,17},{17... | collective-permute-start | bytes 1572872 | tf_op jit(solution)/shard_map/ppermute | solution.py:509
Sparse Core Ops, SparseCore 0:
  9.8 55.7 all-gather.1

commit v2 on v1

--- a/solution.py
+++ b/solution.py
@@ -53,10 +53,7 @@
 def pattern_kernel(
     pos_ref,
     place_ref,
-    own_ref,
-    right_ref,
-    below_ref,
-    diag_ref,
+    ext,
     probe_ref,
     amps_ref,
     th_ref,
@@ -64,7 +61,6 @@
     sel_ref,
     sums_ref,
     part_ref,
-    ext,
     raw,
     amp,
     win,
@@ -73,26 +69,14 @@
     al,
     ye,
     yo,
-    load_sem,
     amp_sem,
 ):
     band = place_ref[0]
     my_col = place_ref[1]
-    loads = []
-    for k, (src, r, c) in enumerate(
-        ((own_ref, 0, 0), (right_ref, 0, N), (below_ref, N, 0), (diag_ref, N, N))
-    ):
-        copy = pltpu.make_async_copy(
-            src, ext.at[:, pl.ds(r, N), pl.ds(c, N)], load_sem.at[k]
-        )
-        copy.start()
-        loads.append(copy)
     for r in range(0, 2 * N, STRIP):
         for q in range(2):
             sums_ref[q, pl.ds(r, STRIP), :] = jnp.zeros((STRIP, 2 * N), jnp.float32)
     part_ref[...] = jnp.zeros_like(part_ref)
-    for copy in loads:
-        copy.wait()
 
     lane = lax.broadcasted_iota(jnp.int32, (STRIP, H), 1)
 
@@ -147,7 +131,7 @@
                 al[k // 2, rows, pl.ds((k % 2) * H, H)] = low
             return 0
 
-        lax.fori_loop(0, N // STRIP, cut, 0)
+        lax.fori_loop(0, N // STRIP, cut, 0, unroll=8)
 
         def right_apply(t):
             for k, out in ((0, ye), (1, yo)):
@@ -179,7 +163,7 @@
                     put(1, dest, cols, a - b)
             return 0
 
-        lax.fori_loop(0, H // STRIP, rows_forward, 0)
+        lax.fori_loop(0, H // STRIP, rows_forward, 0, unroll=4)
         left_apply(1)
         fetch.wait()
         amp[...] = mm(mm(sel_ref[0], raw[...]).astype(jnp.bfloat16), sel_ref[1])
@@ -195,7 +179,7 @@
                 put(k, down, slice(None), im * f)
             return 0
 
-        lax.fori_loop(0, H // STRIP, modulus, 0)
+        lax.fori_loop(0, H // STRIP, modulus, 0, unroll=4)
         left_apply(0)
 
         def rows_back(s, _):
@@ -209,7 +193,7 @@
                     put(1, dest, part, z[:, H:])
             return 0
 
-        lax.fori_loop(0, H // STRIP, rows_back, 0)
+        lax.fori_loop(0, H // STRIP, rows_back, 0, unroll=4)
         right_apply(1)
 
         def finish(s, _):
@@ -235,7 +219,7 @@
                 deposit(sums_ref.at[q], r8 + r0, c128, dr, dc, lane, term[q])
             return 0
 
-        lax.fori_loop(0, N // STRIP, finish, 0)
+        lax.fori_loop(0, N // STRIP, finish, 0, unroll=8)
 
     def visit(i, _):
         j = band * 64 + i
@@ -264,10 +248,11 @@
     sums[spot] = sums[spot] + tall
 
 
-def weights_kernel(pos_ref, place_ref, probe_ref, out_ref, total):
+def weights_kernel(pos_ref, place_ref, probe_ref, out_ref, total, power):
     band = place_ref[0]
     my_col = place_ref[1]
     lane = lax.broadcasted_iota(jnp.int32, (STRIP, H), 1)
+    power[...] = probe_ref[0] * probe_ref[0] + probe_ref[1] * probe_ref[1]
     for r in range(0, 3 * N, STRIP):
         total[pl.ds(r, STRIP), :] = jnp.zeros((STRIP, 3 * N), jnp.float32)
 
@@ -281,19 +266,16 @@
             r8 = (top // 8) * 8
             c128 = pl.multiple_of((left // H) * H, H)
 
-            def strip(s, _):
-                rows = pl.ds(pl.multiple_of(s * STRIP, STRIP), STRIP)
-                halves = []
-                for k in range(2):
-                    cols = pl.ds(k * H, H)
-                    pr, pi = probe_ref[0, k, rows, :], probe_ref[1, k, rows, :]
-                    halves.append(pr * pr + pi * pi)
-                deposit(
-                    total, r8 + s * STRIP, c128, top - r8, left - c128, lane, halves
-                )
-                return 0
-
-            lax.fori_loop(0, N // STRIP, strip, 0)
+            for s in range(N // STRIP):
+                low = top + s * STRIP
+
+                @pl.when((low + STRIP > N) & (low < 2 * N))
+                def _(s=s):
+                    rows = pl.ds(s * STRIP, STRIP)
+                    halves = [power[k, rows, :] for k in range(2)]
+                    deposit(
+                        total, r8 + s * STRIP, c128, top - r8, left - c128, lane, halves
+                    )
 
         return 0
 
@@ -307,7 +289,7 @@
 ANY = pl.BlockSpec(memory_space=pl.ANY)
 
 
-def run_patterns(pos, place, tiles, probe, gathered, high, low, sel):
+def run_patterns(pos, place, ext, probe, gathered, high, low, sel):
     f32, bf16 = jnp.float32, jnp.bfloat16
     return pl.pallas_call(
         pattern_kernel,
@@ -315,10 +297,9 @@
             jax.ShapeDtypeStruct((2, 2 * N, 2 * N), f32),
             jax.ShapeDtypeStruct((3, 2, N, H), f32),
         ),
-        in_specs=[SMEM, SMEM, ANY, ANY, ANY, ANY, VMEM, ANY, VMEM, VMEM, VMEM],
+        in_specs=[SMEM, SMEM, VMEM, VMEM, ANY, VMEM, VMEM, VMEM],
         out_specs=(VMEM, VMEM),
         scratch_shapes=[
-            pltpu.VMEM((2, 2 * N, 2 * N), f32),
             pltpu.VMEM((N, N), bf16),
             pltpu.VMEM((N, N), f32),
             pltpu.VMEM((2, N, N), f32),
@@ -327,12 +308,11 @@
             pltpu.VMEM((2, N, N), bf16),
             pltpu.VMEM((N, N), f32),
             pltpu.VMEM((N, N), f32),
-            pltpu.SemaphoreType.DMA((4,)),
             pltpu.SemaphoreType.DMA,
         ],
         compiler_params=pltpu.CompilerParams(vmem_limit_bytes=40 * 2**20),
         name="patterns",
-    )(pos, place, *tiles, probe, gathered, high, low, sel)
+    )(pos, place, ext, probe, gathered, high, low, sel)
 
 
 def run_weights(pos, place, probe):
@@ -341,7 +321,10 @@
         out_shape=jax.ShapeDtypeStruct((N, N), jnp.float32),
         in_specs=[SMEM, SMEM, VMEM],
         out_specs=VMEM,
-        scratch_shapes=[pltpu.VMEM((3 * N, 3 * N), jnp.float32)],
+        scratch_shapes=[
+            pltpu.VMEM((3 * N, 3 * N), jnp.float32),
+            pltpu.VMEM((2, N, H), jnp.float32),
+        ],
         compiler_params=pltpu.CompilerParams(vmem_limit_bytes=16 * 2**20),
         name="weights",
     )(pos, place, probe)
@@ -350,10 +333,191 @@
 MESH = pl.DeviceIdType.MESH
 
 
-def probe_kernel(
+def whereabouts():
+    row, col = lax.axis_index("row"), lax.axis_index("col")
+    z, y = row // 2, (row % 2) * 2 + (col // 2) % 2
+    x, core = col // 4, col % 2
+
+    def device(z, y, x, core):
+        return (z * 2 + y // 2, x * 4 + (y % 2) * 2 + core)
+
+    return row, col, z, y, x, core, device
+
+
+def greet(peers):
+    barrier = pltpu.get_barrier_semaphore()
+    for peer in peers:
+        pl.semaphore_signal(barrier, inc=1, device_id=peer, device_id_type=MESH)
+    pl.semaphore_wait(barrier, len(peers))
+
+
+class Copies:
+    def __init__(self, send_sem, recv_sem):
+        self.send_sem, self.recv_sem, self.made = send_sem, recv_sem, []
+
+    def make(self, src, dst, peer, k=None):
+        if k is None:
+            k = len(self.made)
+            self.made.append(None)
+        copy = pltpu.make_async_remote_copy(
+            src_ref=src,
+            dst_ref=dst,
+            send_sem=self.send_sem.at[k],
+            recv_sem=self.recv_sem.at[k],
+            device_id=peer,
+            device_id_type=MESH,
+        )
+        self.made[k] = copy
+        return copy, k
+
+    def send(self, src, dst, peer):
+        copy, _ = self.make(src, dst, peer)
+        copy.start()
+        return copy
+
+
+def around(row, col):
+    left, right = lax.rem(col + 15, 16), lax.rem(col + 1, 16)
+    up, down = lax.rem(row + 7, 8), lax.rem(row + 1, 8)
+    return left, right, up, down
+
+
+TOP, END = slice(0, N), slice(N, 2 * N)
+
+
+class Halo:
+    def __init__(self, copies, tile, ext, row, col, core):
+        left, right, up, down = around(row, col)
+        self.core = core
+        self.below = copies.send(tile, ext.at[:, END, TOP], (up, col))
+        self.right = copies.send(tile, ext.at[:, TOP, END], (row, left))
+        corner = ext.at[:, END, END]
+        self.diag, k = copies.make(tile, corner, (up, left))
+        self.onward, _ = copies.make(ext.at[:, END, TOP], corner, (row, left), k)
+
+        @pl.when(core == 0)
+        def _():
+            self.diag.start()
+
+    def pass_on(self):
+        self.below.wait_recv()
+
+        @pl.when(self.core == 1)
+        def _():
+            self.onward.start()
+
+    def finish(self):
+        self.below.wait_send()
+        self.right.wait()
+        self.diag.wait()
+
+
+def start_kernel(obj_ref, amps_ref, ext_ref, all_ref, send_sem, recv_sem, own_sem):
+    row, col, z, y, x, core, device = whereabouts()
+    left, right, up, down = around(row, col)
+    twin = device(z, y, x, 1 - core)
+    beside = device(z, y + 1 - 2 * (y % 2), x, core)
+    ahead, behind = device(z, y, (x + 1) % 4, core), device(z, y, (x + 3) % 4, core)
+    greet(
+        [
+            twin,
+            beside,
+            ahead,
+            behind,
+            (row, left),
+            (row, right),
+            (up, col),
+            (down, col),
+            (up, left),
+            (down, right),
+        ]
+    )
+    copies = Copies(send_sem, recv_sem)
+
+    def block(x, ylo, first=0, count=4):
+        c = (x % 4) * 4 + ylo * 2 + core
+        return all_ref.at[pl.ds(c * 4 + first, count)]
+
+    ylo = y % 2
+    mine, other = block(x, ylo), block(x, 1 - ylo)
+    to_beside = copies.send(amps_ref, mine, beside)
+    to_ahead = copies.send(amps_ref, mine, ahead)
+    to_behind = copies.send(amps_ref, mine, behind)
+    halo = Halo(copies, obj_ref, ext_ref, row, col, core)
+    own = [
+        pltpu.make_async_copy(amps_ref, mine, own_sem.at[0]),
+        pltpu.make_async_copy(obj_ref, ext_ref.at[:, TOP, TOP], own_sem.at[1]),
+    ]
+    for copy in own:
+        copy.start()
+    rest = [copies.send(amps_ref, mine, twin)]
+    to_beside.wait_recv()
+    ahead_2 = copies.send(other, other, ahead)
+    behind_2 = copies.send(other, other, behind)
+    rest.append(copies.send(other, other, twin))
+    far = []
+    for low, high, side in ((to_ahead, to_behind, ylo), (ahead_2, behind_2, 1 - ylo)):
+        low.wait_recv()
+        part = block(x + 3, side, 0, 2)
+        far.append((copies.send(part, part, ahead), block(x + 2, side, 0, 2)))
+        whole = block(x + 3, side)
+        rest.append(copies.send(whole, whole, twin))
+        high.wait_recv()
+        part = block(x + 1, side, 2, 2)
+        far.append((copies.send(part, part, behind), block(x + 2, side, 2, 2)))
+        whole = block(x + 1, side)
+        rest.append(copies.send(whole, whole, twin))
+        if side is ylo:
+            halo.pass_on()
+    for copy, part in far:
+        copy.wait_recv()
+        rest.append(copies.send(part, part, twin))
+    for copy in own:
+        copy.wait()
+    for copy in (to_beside, to_ahead, to_behind, ahead_2, behind_2):
+        copy.wait_send()
+    for copy, _ in far:
+        copy.wait_send()
+    for copy in rest:
+        copy.wait()
+    halo.finish()
+
+
+def run_start(obj, amplitudes):
+    count = 3 + 3 + 1 + 3 + 8 + 4
+    return pl.pallas_call(
+        start_kernel,
+        out_shape=(
+            jax.ShapeDtypeStruct((2, 2 * N, 2 * N), jnp.float32),
+            jax.ShapeDtypeStruct((64, N, N), jnp.bfloat16),
+        ),
+        in_specs=[VMEM, ANY],
+        out_specs=(VMEM, ANY),
+        scratch_shapes=[
+            pltpu.SemaphoreType.DMA((count,)),
+            pltpu.SemaphoreType.DMA((count,)),
+            pltpu.SemaphoreType.DMA((2,)),
+        ],
+        compiler_params=pltpu.CompilerParams(
+            collective_id=1, has_side_effects=True, vmem_limit_bytes=16 * 2**20
+        ),
+        name="start",
+    )(obj, amplitudes)
+
+
+def exchange_kernel(
+    last,
+    sums_ref,
+    weights_ref,
+    ext_ref,
     part_ref,
     old_ref,
+    tile_ref,
     out_ref,
+    from_left,
+    from_above,
+    corner,
+    low,
     pair,
     half,
     from_x,
@@ -364,49 +528,63 @@
     send_sem,
     recv_sem,
 ):
-    row, col = lax.axis_index("row"), lax.axis_index("col")
-    z, y_hi = row // 2, row % 2
-    x, y_lo, core = col // 4, (col // 2) % 2, col % 2
-    y = y_hi * 2 + y_lo
-
-    def device(z, y, x, core):
-        return (z * 2 + y // 2, x * 4 + (y % 2) * 2 + core)
-
+    row, col, z, y, x, core, device = whereabouts()
+    left, right, up, down = around(row, col)
     twin = device(z, y, x, 1 - core)
     on_x = [device(z, y, (x + d) % 4, core) for d in (1, 2, 3)]
     on_y = [device(z, (y + d) % 4, x, core) for d in (1, 2, 3)]
     on_z = [device((z + d) % 4, y, x, core) for d in (1, 2, 3)]
-    barrier = pltpu.get_barrier_semaphore()
-    for peer in (twin, *on_x, *on_y, *on_z):
-        pl.semaphore_signal(barrier, inc=1, device_id=peer, device_id_type=MESH)
-    pl.semaphore_wait(barrier, 10)
-
-    count = [0]
-
-    def send(src, dst, peer):
-        k = count[0]
-        count[0] += 1
-        copy = pltpu.make_async_remote_copy(
-            src_ref=src,
-            dst_ref=dst,
-            send_sem=send_sem.at[k],
-            recv_sem=recv_sem.at[k],
-            device_id=peer,
-            device_id_type=MESH,
-        )
-        copy.start()
-        return copy
-
-    def finish(copies):
-        for copy in copies:
+    greet(
+        [
+            (row, left),
+            (row, right),
+            (up, col),
+            (down, col),
+            (up, left),
+            (down, right),
+            twin,
+            *on_x,
+            *on_y,
+            *on_z,
+        ]
+    )
+    copies = Copies(send_sem, recv_sem)
+
+    def finish(group):
+        for copy in group:
             copy.wait()
 
-    finish([send(part_ref.at[:, 1 - core], pair, twin)])
+    edge = sums_ref.at[:, END, END]
+    inside, k = copies.make(edge, corner, twin)
+    outside, _ = copies.make(edge, corner, (down, right), k)
+
+    @pl.when(core == 0)
+    def _():
+        inside.start()
+
+    on_pair = copies.send(part_ref.at[:, 1 - core], pair, twin)
+    down_sums, k = copies.make(sums_ref.at[:, END, TOP], from_above, (down, col))
+    down_joint, _ = copies.make(low, from_above, (down, col), k)
+
+    @pl.when(core == 0)
+    def _():
+        down_sums.start()
+
+    @pl.when(core == 1)
+    def _():
+        outside.start()
+        inside.wait_recv()
+        low[...] = sums_ref[:, END, TOP] + corner[...]
+        down_joint.start()
+
+    to_right = copies.send(sums_ref.at[:, TOP, END], from_left, (row, right))
+
+    on_pair.wait()
     for q in range(3):
         half[q] = part_ref[q, core] + pair[q]
     finish(
         [
-            send(
+            copies.send(
                 half.at[:, pl.ds(pl.multiple_of((x + d) % 4 * 64, 64), 64), :],
                 from_x.at[d - 1],
                 on_x[d - 1],
@@ -418,7 +596,7 @@
     quarter[...] = (half[:, mine, :] + from_x[0]) + (from_x[1] + from_x[2])
     finish(
         [
-            send(
+            copies.send(
                 quarter.at[:, pl.ds(pl.multiple_of((y + d) % 4 * 16, 16), 16), :],
                 from_y.at[d - 1],
                 on_y[d - 1],
@@ -428,9 +606,31 @@
     )
     mine = pl.ds(pl.multiple_of(y * 16, 16), 16)
     small[...] = (quarter[:, mine, :] + from_y[0]) + (from_y[1] + from_y[2])
-    copies = [send(small, from_z.at[z], peer) for peer in on_z]
+    whole = [copies.send(small, from_z.at[z], peer) for peer in on_z]
     from_z[z] = small[...]
-    finish(copies)
+
+    def object_update():
+        to_right.wait()
+        down_sums.wait()
+
+        @pl.when(core == 0)
+        def _():
+            outside.wait_recv()
+
+        inside.wait_send()
+        for r in range(0, N, STRIP):
+            rows = pl.ds(r, STRIP)
+            scale = 1.0 / (weights_ref[rows, :] + object_regular)
+            for q in range(2):
+                total = sums_ref[q, rows, TOP] + from_left[q, rows, :]
+                total = total + from_above[q, rows, :]
+                total = total + jnp.where(core == 0, corner[q, rows, :], 0.0)
+                tile_ref[q, rows, TOP] = ext_ref[q, rows, TOP] + total * scale
+
+    if not last:
+        object_update()
+        halo = Halo(copies, tile_ref.at[:, TOP, TOP], tile_ref, row, col, core)
+    finish(whole)
     total = (from_z[0] + from_z[1]) + (from_z[2] + from_z[3])
     rows = pl.ds(pl.multiple_of(x * 64 + y * 16, 16), 16)
     for q in range(2):
@@ -438,21 +638,36 @@
             total[2] + probe_regular
         )
     piece = out_ref.at[:, core, rows, :]
-    finish([send(piece, piece, peer) for peer in on_y])
+    finish([copies.send(piece, piece, peer) for peer in on_y])
     piece = out_ref.at[:, core, pl.ds(pl.multiple_of(x * 64, 64), 64), :]
-    finish([send(piece, piece, peer) for peer in on_x])
+    finish([copies.send(piece, piece, peer) for peer in on_x])
     piece = out_ref.at[:, core]
-    finish([send(piece, piece, twin)])
-
-
-def run_probe(partials, probe):
+    to_twin = copies.send(piece, piece, twin)
+    if last:
+        object_update()
+    else:
+        halo.pass_on()
+        halo.finish()
+    to_twin.wait()
+
+
+def run_exchange(last, sums, weights, ext, partials, probe):
     f32 = jnp.float32
+    count = 4 + 9 + (0 if last else 3) + 7
+    tile = (2, N, N) if last else (2, 2 * N, 2 * N)
     return pl.pallas_call(
-        probe_kernel,
-        out_shape=jax.ShapeDtypeStruct((2, 2, N, H), f32),
-        in_specs=[VMEM, VMEM],
-        out_specs=VMEM,
+        functools.partial(exchange_kernel, last),
+        out_shape=(
+            jax.ShapeDtypeStruct(tile, f32),
+            jax.ShapeDtypeStruct((2, 2, N, H), f32),
+        ),
+        in_specs=[VMEM] * 5,
+        out_specs=(VMEM, VMEM),
         scratch_shapes=[
+            pltpu.VMEM((2, N, N), f32),
+            pltpu.VMEM((2, N, N), f32),
+            pltpu.VMEM((2, N, N), f32),
+            pltpu.VMEM((2, N, N), f32),
             pltpu.VMEM((3, N, H), f32),
             pltpu.VMEM((3, N, H), f32),
             pltpu.VMEM((3, 3, 64, H), f32),
@@ -460,66 +675,39 @@
             pltpu.VMEM((3, 3, 16, H), f32),
             pltpu.VMEM((3, 16, H), f32),
             pltpu.VMEM((4, 3, 16, H), f32),
-            pltpu.SemaphoreType.DMA((17,)),
-            pltpu.SemaphoreType.DMA((17,)),
+            pltpu.SemaphoreType.DMA((count,)),
+            pltpu.SemaphoreType.DMA((count,)),
         ],
         compiler_params=pltpu.CompilerParams(
-            collective_id=1, has_side_effects=True, vmem_limit_bytes=16 * 2**20
+            collective_id=3 if last else 2,
+            has_side_effects=True,
+            vmem_limit_bytes=32 * 2**20,
         ),
-        name="probe_sum",
-    )(partials, probe)
-
-
-def shifts(rows, cols, down):
-    near = [(r, r + 1) for r in range(rows - 1)]
-    side = [(c, c + 1) for c in range(cols - 1)]
-    both = [
-        (r * cols + c, (r + 1) * cols + c + 1)
-        for r in range(rows - 1)
-        for c in range(cols - 1)
-    ]
-    if not down:
-        near, side, both = ([(b, a) for a, b in z] for z in (near, side, both))
-    return near, side, both
-
-
-def neighbours(tile, rows, cols):
-    near, side, both = shifts(rows, cols, False)
-    return (
-        tile,
-        lax.ppermute(tile, "col", side),
-        lax.ppermute(tile, "row", near),
-        lax.ppermute(tile, ("row", "col"), both),
-    )
-
-
-def local(rows, cols, obj, probe, amplitudes, positions):
+        name="finish" if last else "exchange",
+    )(sums, weights, ext, partials, probe)
+
+
+def local(obj, probe, amplitudes, positions):
     place = jnp.stack([lax.axis_index("row"), lax.axis_index("col")]).astype(jnp.int32)
     pos = positions.reshape(-1)
     high, low = real_tables()
     sel = order_tables()
-    gathered = lax.all_gather(amplitudes, "col", tiled=True)
-    near, side, both = shifts(rows, cols, True)
-    tile = obj
     illum = jnp.stack([probe[:, :, :H], probe[:, :, H:]], axis=1)
+    weights = run_weights(pos, place, illum)
+    ext, gathered = run_start(obj, amplitudes)
     for sweep in range(ITERS):
-        tiles = neighbours(tile, rows, cols)
-        sums, partials = run_patterns(pos, place, tiles, illum, gathered, high, low, sel)
-        from_left = lax.ppermute(sums[:, :N, N:], "col", side)
-        from_above = lax.ppermute(sums[:, N:, :N], "row", near)
-        from_both = lax.ppermute(sums[:, N:, N:], ("row", "col"), both)
-        weights = run_weights(pos, place, illum)
-        grad = sums[:, :N, :N] + from_left + from_above + from_both
-        tile = tile + grad / (weights + object_regular)[None]
-        illum = run_probe(partials, illum)
-    return tile, jnp.concatenate([illum[:, 0], illum[:, 1]], axis=2)
+        sums, partials = run_patterns(pos, place, ext, illum, gathered, high, low, sel)
+        last = sweep == ITERS - 1
+        ext, illum = run_exchange(last, sums, weights, ext, partials, illum)
+        if not last:
+            weights = run_weights(pos, place, illum)
+    return ext, jnp.concatenate([illum[:, 0], illum[:, 1]], axis=2)
 
 
 def solution(mesh):
-    rows, cols = mesh.shape["row"], mesh.shape["col"]
     placed = (P(None, "row", "col"), P(), P(("row", "col"), None, None), P())
     return jax.shard_map(
-        functools.partial(local, rows, cols),
+        local,
         mesh=mesh,
         in_specs=placed,
         out_specs=(P(None, "row", "col"), P()),

time: 311 us -> 238 us (0.77)
  Pallas kernels: 145 us -> 229 us
  starting transfers between devices: 82.6 us -> 0 us
  waiting for transfers between devices: 63.9 us -> 0 us
  between operations: 14.3 us -> 0.79 us
  local copies, waits for them, and re-layouts: 2.41 us -> 6.29 us
    pallas_call x2 -> x3, Pallas kernels: 91.3 us -> 194 us  [the longest x2 127 us: run_exchange(): pl.pallas_call(functools.partial(exchange_kernel, last), out_shape=(jax.S...]
    ppermute x12 -> x0, starting transfers between devices: 82.6 us -> none  [the longest x2 64.1 us: local(): from_both = lax.ppermute(sums[:, N:, N:], ('row', 'col'), both)]
    ppermute x12 -> x0, waiting for transfers between devices: 45.8 us -> none  [the longest x2 18.1 us: neighbours(): lax.ppermute(tile, ('row', 'col'), both)]
    all_gather x1 -> x0, waiting for transfers between devices: 17.5 us -> none  [local(): gathered = lax.all_gather(amplitudes, 'col', tiled=True)]
    pallas_call x2, Pallas kernels: 38.3 us -> 25.7 us  [run_patterns(): pl.pallas_call(pattern_kernel, out_shape=(jax.ShapeDtypeStruct((2, 2 * N,...]
    pallas_call x2, Pallas kernels: 15.5 us -> 9.87 us  [run_weights(): pl.pallas_call(weights_kernel, out_shape=jax.ShapeDtypeStruct((N, N), jnp...]
    unnamed x9 -> x14, local copies, waits for them, and re-layouts: 0.85 us -> 4.93 us
  transfers between devices with their start and end apart: 13 -> 0, of which waited for: 4 -> 0; matrix products, arithmetic and copies ran while one was open for 1% -> 0% of each run, Pallas kernels for 34% -> 0%
where the time goes in v2:
time: 238 us; the launch traced here: 237 us
  Pallas kernels  229 us (96%)
  local copies, waits for them, and re-layouts  6.29 us (3%)
    pallas_call x2, Pallas kernels, run_exchange(): pl.pallas_call(functools.partial(exchange_kernel, last), out_shape=(jax.S...  127 us
    pallas_call x1, Pallas kernels, run_start(): pl.pallas_call(start_kernel, out_shape=(jax.ShapeDtypeStruct((2, 2 * N, 2...  66.4 us
    pallas_call x2, Pallas kernels, run_patterns(): pl.pallas_call(pattern_kernel, out_shape=(jax.ShapeDtypeStruct((2, 2 * N,...  25.7 us
    pallas_call x2, Pallas kernels, run_weights(): pl.pallas_call(weights_kernel, out_shape=jax.ShapeDtypeStruct((N, N), jnp...  9.87 us
    unnamed x14, local copies, waits for them, and re-layouts  4.93 us

profile of v2, /device:TPU:1, one launch (start us, length us, event | category | flops | bytes accessed | tf_op | source)
XLA Modules:
  0.0 237.2 jit_solution(3809774979607346685)
XLA Ops:
  0.6 0.0 copy-start.5
  0.6 0.0 copy-start.4
  0.7 0.1 pad_add_fusion.place_ref
  0.7 0.9 copy.9
  1.6 0.0 copy-start.1
  1.6 0.0 copy-start.2
  1.7 0.0 copy-start.3
  1.7 0.2 reshape.7.pos_ref
  1.8 1.2 slice_bitcast_fusion.3
  3.0 4.9 %weights.2.weights_ref = f32[256,256]{1,0:T(8,128)S(1)} custom-call(s32[1024]{0:T(1024)S(1)} %reshape.7.pos_ref, s32[2]{0:T(128)S(1)} %pad_add_fusion.place_ref, f32[2,2,256,128]{3,2,1,0:T(8,128)S(1)} %pad_maximum_fusion.probe_ref.old_ref), custom_call_target="tpu_custom_call" | custom-call | tf_op jit(solution)/shard_map/weights/pallas_call | solution.py:319
  8.0 0.0 copy-done.5
  8.0 0.0 copy-done.4
  8.0 66.4 %start.1 = (f32[2,512,512]{2,1,0:T(8,128)S(1)}, bf16[64,256,256]{2,1,0:T(8,128)(2,1)S(1)}) custom-call(f32[2,256,256]{2,1,0:T(8,128)S(1)} %copy-done.4, bf16[4,256,256]{2,1,0:T(8,128)(2,1)S(1)} %copy-done.5), custom_call_target="tpu_custom_call" | custom-call | tf_op jit(solution)/shard_map/start/pallas_call | solution.py:488
  74.4 0.0 copy-start
  74.4 3.2 %copy-done = bf16[64,256,256]{2,1,0:T(8,128)(2,1)} copy-done((bf16[64,256,256]{2,1,0:T(8,128)(2,1)}, bf16[64,256,256]{2,1,0:T(8,128)(2,1)S(1)}, u32[]{:S(2)}) %copy-start) | copy-done | bytes 8388632
  77.6 0.0 copy-done.1
  77.6 0.0 copy-done.2
  77.6 0.0 copy-done.3
  77.6 12.8 %patterns.2 = (f32[2,512,512]{2,1,0:T(8,128)S(1)}, f32[3,2,256,128]{3,2,1,0:T(8,128)S(1)}) custom-call(s32[1024]{0:T(1024)S(1)} %reshape.7.pos_ref, s32[2]{0:T(128)S(1)} %pad_add_fusion.place_ref, f32[2,512,512]{2,1,0:T(8,128)S(1)} %get-tuple-element.12.ext.ext_ref, f32[2,2,256,128]{3,2,1,0:T(8,128)S(1)} %pad_maximum_fusion.probe_ref.old_ref, ...), custom_call_target="tpu_custom_call" | custom-call | tf_op jit(solution)/shard_map/patterns/pallas_call | solution.py:294
  90.5 69.6 %exchange.1 = (f32[2,512,512]{2,1,0:T(8,128)S(1)}, f32[2,2,256,128]{3,2,1,0:T(8,128)S(1)}) custom-call(f32[2,512,512]{2,1,0:T(8,128)S(1)} %get-tuple-element.14.sums_ref, f32[256,256]{1,0:T(8,128)S(1)} %weights.2.weights_ref, f32[2,512,512]{2,1,0:T(8,128)S(1)} %get-tuple-element.12.ext.ext_ref, f32[3,2,256,128]{3,2,1,0:T(8,128)S(1)} %get-tuple-element.15.part_ref, ...), custom_call_target="tpu_custom_call" | custom-call | tf_op jit(solution)/shard_map/exchange/pallas_call | solution.py:658
  160.1 12.8 %patterns.3 = (f32[2,512,512]{2,1,0:T(8,128)S(1)}, f32[3,2,256,128]{3,2,1,0:T(8,128)S(1)}) custom-call(s32[1024]{0:T(1024)S(1)} %reshape.7.pos_ref, s32[2]{0:T(128)S(1)} %pad_add_fusion.place_ref, f32[2,512,512]{2,1,0:T(8,128)S(1)} %get-tuple-element.16.ext.ext_ref, f32[2,2,256,128]{3,2,1,0:T(8,128)S(1)} %get-tuple-element.17.probe_ref.old_ref, ...), custom_call_target="tpu_custom_call" | custom-call | tf_op jit(solution)/shard_map/patterns/pallas_call | solution.py:294
  173.0 4.9 %weights.3.weights_ref = f32[256,256]{1,0:T(8,128)S(1)} custom-call(s32[1024]{0:T(1024)S(1)} %reshape.7.pos_ref, s32[2]{0:T(128)S(1)} %pad_add_fusion.place_ref, f32[2,2,256,128]{3,2,1,0:T(8,128)S(1)} %get-tuple-element.17.probe_ref.old_ref), custom_call_target="tpu_custom_call" | custom-call | tf_op jit(solution)/shard_map/weights/pallas_call | solution.py:319
  177.9 57.6 %finish.1 = (f32[2,256,256]{2,1,0:T(8,128)S(1)}, f32[2,2,256,128]{3,2,1,0:T(8,128)S(1)}) custom-call(f32[2,512,512]{2,1,0:T(8,128)S(1)} %get-tuple-element.18.sums_ref, f32[256,256]{1,0:T(8,128)S(1)} %weights.3.weights_ref, f32[2,512,512]{2,1,0:T(8,128)S(1)} %get-tuple-element.16.ext.ext_ref, f32[3,2,256,128]{3,2,1,0:T(8,128)S(1)} %get-tuple-element.19.part_ref, ...), custom_call_target="tpu_custom_call" | custom-call | tf_op jit(solution)/shard_map/finish/pallas_call | solution.py:658
  235.6 0.8 pad_maximum_fusion.1
  236.4 0.8 copy.14
  (3 shorter events, 0.1 us)
Async XLA Ops:
  0.6 7.4 %copy-start.5 = (bf16[4,256,256]{2,1,0:T(8,128)(2,1)S(1)}, bf16[4,256,256]{2,1,0:T(8,128)(2,1)}, u32[]{:S(2)}) copy-start(bf16[4,256,256]{2,1,0:T(8,128)(2,1)} %amps_ref.1) | copy-start | bytes 1572868
  0.6 7.4 %copy-start.4 = (f32[2,256,256]{2,1,0:T(8,128)S(1)}, f32[2,256,256]{2,1,0:T(8,128)}, u32[]{:S(2)}) copy-start(f32[2,256,256]{2,1,0:T(8,128)} %obj_ref.1) | copy-start | bytes 1572868
  1.6 76.0 %copy-start.1 = (bf16[4,256,256]{2,1,0:T(8,128)(2,1)S(1)}, bf16[4,256,256]{2,1,0:T(8,128)(2,1)}, u32[]{:S(2)}) copy-start(bf16[4,256,256]{2,1,0:T(8,128)(2,1)} %constant.19.tl_ref) | copy-start | bytes 1572868
  1.6 76.0 %copy-start.2 = (bf16[4,256,256]{2,1,0:T(8,128)(2,1)S(1)}, bf16[4,256,256]{2,1,0:T(8,128)(2,1)}, u32[]{:S(2)}) copy-start(bf16[4,256,256]{2,1,0:T(8,128)(2,1)} %constant.16.th_ref) | copy-start | bytes 1572868
  1.7 76.0 %copy-start.3 = (bf16[2,256,256]{2,1,0:T(8,128)(2,1)S(1)}, bf16[2,256,256]{2,1,0:T(8,128)(2,1)}, u32[]{:S(2)}) copy-start(bf16[2,256,256]{2,1,0:T(8,128)(2,1)} %constant.20.sel_ref) | copy-start | bytes 786436
  74.4 3.2 %copy-start = (bf16[64,256,256]{2,1,0:T(8,128)(2,1)}, bf16[64,256,256]{2,1,0:T(8,128)(2,1)S(1)}, u32[]{:S(2)}) copy-start(bf16[64,256,256]{2,1,0:T(8,128)(2,1)S(1)} %get-tuple-element.13.amps_ref) | copy-start | bytes 25165828

commit v3 on v2

--- a/solution.py
+++ b/solution.py
@@ -14,6 +14,8 @@
 probe_regular = 1.0
 
 N = 256
+NEAR = 32
+FAR = 4096
 H = 128
 STRIP = 32
 
@@ -51,6 +53,7 @@
 
 
 def pattern_kernel(
+    first,
     pos_ref,
     place_ref,
     ext,
@@ -61,6 +64,7 @@
     sel_ref,
     sums_ref,
     part_ref,
+    near_ref,
     raw,
     amp,
     win,
@@ -232,6 +236,25 @@
         return 0
 
     lax.fori_loop(0, 64, visit, 0)
+    if not first:
+        return
+
+    for k in range(2 * NEAR):
+        near_ref[k] = FAR
+
+    def note(j, found):
+        dy = pos_ref[2 * j] - band * N
+        dx = pos_ref[2 * j + 1] - my_col * N
+        reach = (dy > -N) & (dx > -N) & (dy < N) & (dx < N)
+
+        @pl.when(reach)
+        def _():
+            near_ref[2 * found] = dy
+            near_ref[2 * found + 1] = dx
+
+        return found + reach.astype(jnp.int32)
+
+    lax.fori_loop(jnp.maximum(band - 1, 0) * 64, (band + 1) * 64, note, 0)
 
 
 def deposit(sums, row, col, dr, dc, lane, halves):
@@ -248,57 +271,22 @@
     sums[spot] = sums[spot] + tall
 
 
-def weights_kernel(pos_ref, place_ref, probe_ref, out_ref, total, power):
-    band = place_ref[0]
-    my_col = place_ref[1]
-    lane = lax.broadcasted_iota(jnp.int32, (STRIP, H), 1)
-    power[...] = probe_ref[0] * probe_ref[0] + probe_ref[1] * probe_ref[1]
-    for r in range(0, 3 * N, STRIP):
-        total[pl.ds(r, STRIP), :] = jnp.zeros((STRIP, 3 * N), jnp.float32)
-
-    def visit(j, _):
-        y, x = pos_ref[2 * j], pos_ref[2 * j + 1]
-        top = y - band * N + N
-        left = x - my_col * N + N
-
-        @pl.when((top > 0) & (left > 0) & (top < 2 * N) & (left < 2 * N))
-        def _():
-            r8 = (top // 8) * 8
-            c128 = pl.multiple_of((left // H) * H, H)
-
-            for s in range(N // STRIP):
-                low = top + s * STRIP
-
-                @pl.when((low + STRIP > N) & (low < 2 * N))
-                def _(s=s):
-                    rows = pl.ds(s * STRIP, STRIP)
-                    halves = [power[k, rows, :] for k in range(2)]
-                    deposit(
-                        total, r8 + s * STRIP, c128, top - r8, left - c128, lane, halves
-                    )
-
-        return 0
-
-    first = jnp.maximum(band - 1, 0) * 64
-    lax.fori_loop(first, (band + 1) * 64, visit, 0)
-    out_ref[...] = total[N : 2 * N, N : 2 * N]
-
-
 SMEM = pl.BlockSpec(memory_space=pltpu.SMEM)
 VMEM = pl.BlockSpec(memory_space=pltpu.VMEM)
-ANY = pl.BlockSpec(memory_space=pl.ANY)
-
-
-def run_patterns(pos, place, ext, probe, gathered, high, low, sel):
+ANY = pl.BlockSpec(memory_space=pltpu.HBM)
+
+
+def run_patterns(first, pos, place, ext, probe, gathered, high, low, sel):
     f32, bf16 = jnp.float32, jnp.bfloat16
     return pl.pallas_call(
-        pattern_kernel,
+        functools.partial(pattern_kernel, first),
         out_shape=(
             jax.ShapeDtypeStruct((2, 2 * N, 2 * N), f32),
             jax.ShapeDtypeStruct((3, 2, N, H), f32),
+            jax.ShapeDtypeStruct((2 * NEAR,), jnp.int32),
         ),
         in_specs=[SMEM, SMEM, VMEM, VMEM, ANY, VMEM, VMEM, VMEM],
-        out_specs=(VMEM, VMEM),
+        out_specs=(VMEM, VMEM, SMEM),
         scratch_shapes=[
             pltpu.VMEM((N, N), bf16),
             pltpu.VMEM((N, N), f32),
@@ -315,21 +303,6 @@
     )(pos, place, ext, probe, gathered, high, low, sel)
 
 
-def run_weights(pos, place, probe):
-    return pl.pallas_call(
-        weights_kernel,
-        out_shape=jax.ShapeDtypeStruct((N, N), jnp.float32),
-        in_specs=[SMEM, SMEM, VMEM],
-        out_specs=VMEM,
-        scratch_shapes=[
-            pltpu.VMEM((3 * N, 3 * N), jnp.float32),
-            pltpu.VMEM((2, N, H), jnp.float32),
-        ],
-        compiler_params=pltpu.CompilerParams(vmem_limit_bytes=16 * 2**20),
-        name="weights",
-    )(pos, place, probe)
-
-
 MESH = pl.DeviceIdType.MESH
 
 
@@ -389,27 +362,29 @@
     def __init__(self, copies, tile, ext, row, col, core):
         left, right, up, down = around(row, col)
         self.core = core
-        self.below = copies.send(tile, ext.at[:, END, TOP], (up, col))
-        self.right = copies.send(tile, ext.at[:, TOP, END], (row, left))
+        self.below, _ = copies.make(tile, ext.at[:, END, TOP], (up, col))
+        self.right, _ = copies.make(tile, ext.at[:, TOP, END], (row, left))
         corner = ext.at[:, END, END]
         self.diag, k = copies.make(tile, corner, (up, left))
         self.onward, _ = copies.make(ext.at[:, END, TOP], corner, (row, left), k)
 
-        @pl.when(core == 0)
+    def start_sides(self):
+        self.right.start()
+
+        @pl.when(self.core == 0)
         def _():
             self.diag.start()
 
-    def pass_on(self):
+    def finish(self):
         self.below.wait_recv()
 
         @pl.when(self.core == 1)
         def _():
             self.onward.start()
 
-    def finish(self):
         self.below.wait_send()
         self.right.wait()
-        self.diag.wait()
+        self.onward.wait()
 
 
 def start_kernel(obj_ref, amps_ref, ext_ref, all_ref, send_sem, recv_sem, own_sem):
@@ -444,6 +419,8 @@
     to_ahead = copies.send(amps_ref, mine, ahead)
     to_behind = copies.send(amps_ref, mine, behind)
     halo = Halo(copies, obj_ref, ext_ref, row, col, core)
+    halo.below.start()
+    halo.start_sides()
     own = [
         pltpu.make_async_copy(amps_ref, mine, own_sem.at[0]),
         pltpu.make_async_copy(obj_ref, ext_ref.at[:, TOP, TOP], own_sem.at[1]),
@@ -467,8 +444,6 @@
         far.append((copies.send(part, part, behind), block(x + 2, side, 2, 2)))
         whole = block(x + 1, side)
         rest.append(copies.send(whole, whole, twin))
-        if side is ylo:
-            halo.pass_on()
     for copy, part in far:
         copy.wait_recv()
         rest.append(copies.send(part, part, twin))
@@ -508,7 +483,7 @@
 def exchange_kernel(
     last,
     sums_ref,
-    weights_ref,
+    near_ref,
     ext_ref,
     part_ref,
     old_ref,
@@ -522,9 +497,12 @@
     half,
     from_x,
     quarter,
+    from_z,
+    small,
     from_y,
-    small,
-    from_z,
+    weights,
+    power_high,
+    power_low,
     send_sem,
     recv_sem,
 ):
@@ -554,60 +532,83 @@
         for copy in group:
             copy.wait()
 
+    def add_weights(start, stop):
+        gap = lax.broadcasted_iota(jnp.int32, (N, N), 0) - lax.broadcasted_iota(
+            jnp.int32, (N, N), 1
+        )
+
+        def add(i, _):
+            dy, dx = near_ref[2 * i], near_ref[2 * i + 1]
+            to_row = jnp.where(gap == dy, 1.0, 0.0).astype(jnp.bfloat16)
+            to_col = jnp.where(gap == -dx, 1.0, 0.0).astype(jnp.bfloat16)
+            a = mm(power_high[...], to_col).astype(jnp.bfloat16)
+            b = mm(power_low[...], to_col).astype(jnp.bfloat16)
+            weights[...] += mm(to_row, a) + mm(to_row, b)
+            return 0
+
+        lax.fori_loop(start, stop, add, 0)
+
+    on_pair = copies.send(part_ref.at[:, 1 - core], pair, twin)
     edge = sums_ref.at[:, END, END]
     inside, k = copies.make(edge, corner, twin)
     outside, _ = copies.make(edge, corner, (down, right), k)
+    down_sums, k = copies.make(sums_ref.at[:, END, TOP], from_above, (down, col))
+    down_joint, _ = copies.make(low, from_above, (down, col), k)
+    to_right, _ = copies.make(sums_ref.at[:, TOP, END], from_left, (row, right))
 
     @pl.when(core == 0)
     def _():
         inside.start()
-
-    on_pair = copies.send(part_ref.at[:, 1 - core], pair, twin)
-    down_sums, k = copies.make(sums_ref.at[:, END, TOP], from_above, (down, col))
-    down_joint, _ = copies.make(low, from_above, (down, col), k)
-
-    @pl.when(core == 0)
+        down_sums.start()
+
+    weights[...] = jnp.zeros((N, N), jnp.float32)
+    for k in range(2):
+        cols = pl.ds(k * H, H)
+        power = old_ref[0, k] * old_ref[0, k] + old_ref[1, k] * old_ref[1, k]
+        power_high[:, cols], power_low[:, cols] = split(power)
+    on_pair.wait()
+    for q in range(3):
+        half[q] = part_ref[q, core] + pair[q]
+    group = [
+        copies.send(
+            half.at[:, pl.ds(pl.multiple_of((x + d) % 4 * 64, 64), 64), :],
+            from_x.at[d - 1],
+            on_x[d - 1],
+        )
+        for d in (1, 2, 3)
+    ]
+
+    @pl.when(core == 1)
     def _():
-        down_sums.start()
+        inside.wait_recv()
+        low[...] = sums_ref[:, END, TOP] + corner[...]
+        down_joint.start()
+
+    add_weights(0, 16)
+    finish(group)
+    mine = pl.ds(pl.multiple_of(x * 64, 64), 64)
+    quarter[...] = (half[:, mine, :] + from_x[0]) + (from_x[1] + from_x[2])
+    group = [
+        copies.send(
+            quarter.at[:, pl.ds(pl.multiple_of((z + d) % 4 * 16, 16), 16), :],
+            from_z.at[d - 1],
+            on_z[d - 1],
+        )
+        for d in (1, 2, 3)
+    ]
 
     @pl.when(core == 1)
     def _():
         outside.start()
-        inside.wait_recv()
-        low[...] = sums_ref[:, END, TOP] + corner[...]
-        down_joint.start()
-
-    to_right = copies.send(sums_ref.at[:, TOP, END], from_left, (row, right))
-
-    on_pair.wait()
-    for q in range(3):
-        half[q] = part_ref[q, core] + pair[q]
-    finish(
-        [
-            copies.send(
-                half.at[:, pl.ds(pl.multiple_of((x + d) % 4 * 64, 64), 64), :],
-                from_x.at[d - 1],
-                on_x[d - 1],
-            )
-            for d in (1, 2, 3)
-        ]
-    )
-    mine = pl.ds(pl.multiple_of(x * 64, 64), 64)
-    quarter[...] = (half[:, mine, :] + from_x[0]) + (from_x[1] + from_x[2])
-    finish(
-        [
-            copies.send(
-                quarter.at[:, pl.ds(pl.multiple_of((y + d) % 4 * 16, 16), 16), :],
-                from_y.at[d - 1],
-                on_y[d - 1],
-            )
-            for d in (1, 2, 3)
-        ]
-    )
-    mine = pl.ds(pl.multiple_of(y * 16, 16), 16)
-    small[...] = (quarter[:, mine, :] + from_y[0]) + (from_y[1] + from_y[2])
-    whole = [copies.send(small, from_z.at[z], peer) for peer in on_z]
-    from_z[z] = small[...]
+
+    to_right.start()
+    add_weights(16, 24)
+    finish(group)
+    mine = pl.ds(pl.multiple_of(z * 16, 16), 16)
+    small[...] = (quarter[:, mine, :] + from_z[0]) + (from_z[1] + from_z[2])
+    group = [copies.send(small, from_y.at[y], peer) for peer in on_y]
+    from_y[y] = small[...]
+    add_weights(24, 32)
 
     def object_update():
         to_right.wait()
@@ -617,10 +618,10 @@
         def _():
             outside.wait_recv()
 
-        inside.wait_send()
+        outside.wait_send()
         for r in range(0, N, STRIP):
             rows = pl.ds(r, STRIP)
-            scale = 1.0 / (weights_ref[rows, :] + object_regular)
+            scale = 1.0 / (weights[rows, :] + object_regular)
             for q in range(2):
                 total = sums_ref[q, rows, TOP] + from_left[q, rows, :]
                 total = total + from_above[q, rows, :]
@@ -630,28 +631,31 @@
     if not last:
         object_update()
         halo = Halo(copies, tile_ref.at[:, TOP, TOP], tile_ref, row, col, core)
-    finish(whole)
-    total = (from_z[0] + from_z[1]) + (from_z[2] + from_z[3])
-    rows = pl.ds(pl.multiple_of(x * 64 + y * 16, 16), 16)
+        halo.below.start()
+    finish(group)
+    total = (from_y[0] + from_y[1]) + (from_y[2] + from_y[3])
+    rows = pl.ds(pl.multiple_of(x * 64 + z * 16, 16), 16)
     for q in range(2):
         out_ref[q, core, rows, :] = old_ref[q, core, rows, :] + total[q] / (
             total[2] + probe_regular
         )
     piece = out_ref.at[:, core, rows, :]
-    finish([copies.send(piece, piece, peer) for peer in on_y])
+    finish([copies.send(piece, piece, peer) for peer in on_z])
     piece = out_ref.at[:, core, pl.ds(pl.multiple_of(x * 64, 64), 64), :]
-    finish([copies.send(piece, piece, peer) for peer in on_x])
-    piece = out_ref.at[:, core]
-    to_twin = copies.send(piece, piece, twin)
+    group = [copies.send(piece, piece, peer) for peer in on_x]
     if last:
         object_update()
     else:
-        halo.pass_on()
+        halo.start_sides()
+    finish(group)
+    piece = out_ref.at[:, core]
+    to_twin = copies.send(piece, piece, twin)
+    if not last:
         halo.finish()
     to_twin.wait()
 
 
-def run_exchange(last, sums, weights, ext, partials, probe):
+def run_exchange(last, sums, near, ext, partials, probe):
     f32 = jnp.float32
     count = 4 + 9 + (0 if last else 3) + 7
     tile = (2, N, N) if last else (2, 2 * N, 2 * N)
@@ -661,7 +665,7 @@
             jax.ShapeDtypeStruct(tile, f32),
             jax.ShapeDtypeStruct((2, 2, N, H), f32),
         ),
-        in_specs=[VMEM] * 5,
+        in_specs=[VMEM, SMEM, VMEM, VMEM, VMEM],
         out_specs=(VMEM, VMEM),
         scratch_shapes=[
             pltpu.VMEM((2, N, N), f32),
@@ -675,6 +679,9 @@
             pltpu.VMEM((3, 3, 16, H), f32),
             pltpu.VMEM((3, 16, H), f32),
             pltpu.VMEM((4, 3, 16, H), f32),
+            pltpu.VMEM((N, N), f32),
+            pltpu.VMEM((N, N), jnp.bfloat16),
+            pltpu.VMEM((N, N), jnp.bfloat16),
             pltpu.SemaphoreType.DMA((count,)),
             pltpu.SemaphoreType.DMA((count,)),
         ],
@@ -684,7 +691,7 @@
             vmem_limit_bytes=32 * 2**20,
         ),
         name="finish" if last else "exchange",
-    )(sums, weights, ext, partials, probe)
+    )(sums, near, ext, partials, probe)
 
 
 def local(obj, probe, amplitudes, positions):
@@ -693,14 +700,16 @@
     high, low = real_tables()
     sel = order_tables()
     illum = jnp.stack([probe[:, :, :H], probe[:, :, H:]], axis=1)
-    weights = run_weights(pos, place, illum)
     ext, gathered = run_start(obj, amplitudes)
+    near = None
     for sweep in range(ITERS):
-        sums, partials = run_patterns(pos, place, ext, illum, gathered, high, low, sel)
-        last = sweep == ITERS - 1
-        ext, illum = run_exchange(last, sums, weights, ext, partials, illum)
-        if not last:
-            weights = run_weights(pos, place, illum)
+        sums, partials, listed = run_patterns(
+            sweep == 0, pos, place, ext, illum, gathered, high, low, sel
+        )
+        near = listed if sweep == 0 else near
+        ext, illum = run_exchange(
+            sweep == ITERS - 1, sums, near, ext, partials, illum
+        )
     return ext, jnp.concatenate([illum[:, 0], illum[:, 1]], axis=2)
 
 

time: 238 us -> 216 us (0.908)
  Pallas kernels: 229 us -> 208 us
    pallas_call x4 -> x2, Pallas kernels: 35.6 us -> 27.4 us  [run_patterns(): pl.pallas_call(functools.partial(pattern_kernel, first), out_shape=(jax.S...]
    pallas_call x1, Pallas kernels: 66.4 us -> 59 us  [run_start(): pl.pallas_call(start_kernel, out_shape=(jax.ShapeDtypeStruct((2, 2 * N, 2...]
    pallas_call x2, Pallas kernels: 127 us -> 121 us  [run_exchange(): pl.pallas_call(functools.partial(exchange_kernel, last), out_shape=(jax.S...]
where the time goes in v3:
time: 216 us
  Pallas kernels  208 us (96%)
  local copies, waits for them, and re-layouts  6.27 us (3%)
    pallas_call x2, Pallas kernels, run_exchange(): pl.pallas_call(functools.partial(exchange_kernel, last), out_shape=(jax.S...  121 us
    pallas_call x1, Pallas kernels, run_start(): pl.pallas_call(start_kernel, out_shape=(jax.ShapeDtypeStruct((2, 2 * N, 2...  59 us
    pallas_call x2, Pallas kernels, run_patterns(): pl.pallas_call(functools.partial(pattern_kernel, first), out_shape=(jax.S...  27.4 us
    unnamed x14, local copies, waits for them, and re-layouts  5 us

profile of v3, /device:TPU:1, one launch (start us, length us, event | category | flops | bytes accessed | tf_op | source)
XLA Modules:
  0.0 215.8 jit_solution(4627435240122824877)
XLA Ops:
  0.6 0.0 copy-start.3
  0.6 0.0 copy-start.1
  0.7 0.0 copy-start.2
  0.7 0.0 copy-start.5
  0.7 0.0 copy-start.4
  0.7 0.1 pad_add_fusion.place_ref
  0.8 1.0 copy.9
  1.7 0.2 reshape.7.pos_ref
  1.9 1.1 slice_bitcast_fusion.3
  3.0 0.0 copy-done.5
  3.0 0.0 copy-done.4
  3.0 59.0 %start.1 = (f32[2,512,512]{2,1,0:T(8,128)S(1)}, bf16[64,256,256]{2,1,0:T(8,128)(2,1)S(1)}) custom-call(f32[2,256,256]{2,1,0:T(8,128)S(1)} %copy-done.4, bf16[4,256,256]{2,1,0:T(8,128)(2,1)S(1)} %copy-done.5), custom_call_target="tpu_custom_call" | custom-call | tf_op jit(solution)/shard_map/start/pallas_call | solution.py:463
  62.1 0.0 copy-start
  62.1 3.2 %copy-done = bf16[64,256,256]{2,1,0:T(8,128)(2,1)} copy-done((bf16[64,256,256]{2,1,0:T(8,128)(2,1)}, bf16[64,256,256]{2,1,0:T(8,128)(2,1)S(1)}, u32[]{:S(2)}) %copy-start) | copy-done | bytes 8388632
  65.3 0.0 copy-done.3
  65.3 0.0 copy-done.1
  65.3 0.0 copy-done.2
  65.3 14.0 %patterns.2 = (f32[2,512,512]{2,1,0:T(8,128)S(1)}, f32[3,2,256,128]{3,2,1,0:T(8,128)S(1)}, s32[64]{0:T(128)S(1)}) custom-call(s32[1024]{0:T(1024)S(1)} %reshape.7.pos_ref, s32[2]{0:T(128)S(1)} %pad_add_fusion.place_ref, f32[2,512,512]{2,1,0:T(8,128)S(1)} %get-tuple-element.13.ext.ext_ref, f32[2,2,256,128]{3,2,1,0:T(8,128)S(1)} %pad_maximum_fusion.probe_ref.old_ref, ...), custom_call_target="tpu_custom_call" | custom-call | tf_op jit(solution)/shard_map/patterns/pallas_call | solution.py:281
  79.3 55.5 %exchange.1 = (f32[2,512,512]{2,1,0:T(8,128)S(1)}, f32[2,2,256,128]{3,2,1,0:T(8,128)S(1)}) custom-call(f32[2,512,512]{2,1,0:T(8,128)S(1)} %get-tuple-element.15.sums_ref, s32[64]{0:T(128)S(1)} %get-tuple-element.16.near_ref, f32[2,512,512]{2,1,0:T(8,128)S(1)} %get-tuple-element.13.ext.ext_ref, f32[3,2,256,128]{3,2,1,0:T(8,128)S(1)} %get-tuple-element.17.part_ref, ...), custom_call_target="tpu_custom_call" | custom-call | tf_op jit(solution)/shard_map/exchange/pallas_call | solution.py:662
  134.8 13.4 %patterns.3 = (f32[2,512,512]{2,1,0:T(8,128)S(1)}, f32[3,2,256,128]{3,2,1,0:T(8,128)S(1)}, s32[64]{0:T(128)}) custom-call(s32[1024]{0:T(1024)S(1)} %reshape.7.pos_ref, s32[2]{0:T(128)S(1)} %pad_add_fusion.place_ref, f32[2,512,512]{2,1,0:T(8,128)S(1)} %get-tuple-element.18.ext.ext_ref, f32[2,2,256,128]{3,2,1,0:T(8,128)S(1)} %get-tuple-element.19.probe_ref.old_ref, ...), custom_call_target="tpu_custom_call" | custom-call | tf_op jit(solution)/shard_map/patterns/pallas_call | solution.py:281
  148.2 66.0 %finish.1 = (f32[2,256,256]{2,1,0:T(8,128)S(1)}, f32[2,2,256,128]{3,2,1,0:T(8,128)S(1)}) custom-call(f32[2,512,512]{2,1,0:T(8,128)S(1)} %get-tuple-element.20.sums_ref, s32[64]{0:T(128)S(1)} %get-tuple-element.16.near_ref, f32[2,512,512]{2,1,0:T(8,128)S(1)} %get-tuple-element.18.ext.ext_ref, f32[3,2,256,128]{3,2,1,0:T(8,128)S(1)} %get-tuple-element.21.part_ref, ...), custom_call_target="tpu_custom_call" | custom-call | tf_op jit(solution)/shard_map/finish/pallas_call | solution.py:662
  214.2 0.8 pad_maximum_fusion.1
  215.0 0.8 copy.14
  (3 shorter events, 0.1 us)
Async XLA Ops:
  0.6 64.7 %copy-start.3 = (bf16[2,256,256]{2,1,0:T(8,128)(2,1)S(1)}, bf16[2,256,256]{2,1,0:T(8,128)(2,1)}, u32[]{:S(2)}) copy-start(bf16[2,256,256]{2,1,0:T(8,128)(2,1)} %constant.20.sel_ref) | copy-start | bytes 786436
  0.6 64.7 %copy-start.1 = (bf16[4,256,256]{2,1,0:T(8,128)(2,1)S(1)}, bf16[4,256,256]{2,1,0:T(8,128)(2,1)}, u32[]{:S(2)}) copy-start(bf16[4,256,256]{2,1,0:T(8,128)(2,1)} %constant.19.tl_ref) | copy-start | bytes 1572868
  0.7 64.6 %copy-start.2 = (bf16[4,256,256]{2,1,0:T(8,128)(2,1)S(1)}, bf16[4,256,256]{2,1,0:T(8,128)(2,1)}, u32[]{:S(2)}) copy-start(bf16[4,256,256]{2,1,0:T(8,128)(2,1)} %constant.16.th_ref) | copy-start | bytes 1572868
  0.7 2.4 %copy-start.5 = (bf16[4,256,256]{2,1,0:T(8,128)(2,1)S(1)}, bf16[4,256,256]{2,1,0:T(8,128)(2,1)}, u32[]{:S(2)}) copy-start(bf16[4,256,256]{2,1,0:T(8,128)(2,1)} %amps_ref.1) | copy-start | bytes 1572868
  0.7 2.4 %copy-start.4 = (f32[2,256,256]{2,1,0:T(8,128)S(1)}, f32[2,256,256]{2,1,0:T(8,128)}, u32[]{:S(2)}) copy-start(f32[2,256,256]{2,1,0:T(8,128)} %obj_ref.1) | copy-start | bytes 1572868
  62.1 3.2 %copy-start = (bf16[64,256,256]{2,1,0:T(8,128)(2,1)}, bf16[64,256,256]{2,1,0:T(8,128)(2,1)S(1)}, u32[]{:S(2)}) copy-start(bf16[64,256,256]{2,1,0:T(8,128)(2,1)S(1)} %get-tuple-element.14.amps_ref) | copy-start | bytes 25165828

commit v4 on v3

--- a/solution.py
+++ b/solution.py
@@ -65,15 +65,8 @@
     sums_ref,
     part_ref,
     near_ref,
-    raw,
-    amp,
-    win,
-    psi,
-    ah,
-    al,
-    ye,
-    yo,
-    amp_sem,
+    todo,
+    *work,
 ):
     band = place_ref[0]
     my_col = place_ref[1]
@@ -84,16 +77,15 @@
 
     lane = lax.broadcasted_iota(jnp.int32, (STRIP, H), 1)
 
-    def process(j, top, left):
-        fetch = pltpu.make_async_copy(amps_ref.at[j], raw, amp_sem)
-        fetch.start()
+    def process(spaces, j, top, left, valid):
+        amp, win, psi, ah, al, ye, yo = spaces
         r8 = pl.multiple_of((top // 8) * 8, 8)
         dr = top - r8
         c128 = pl.multiple_of((left // H) * H, H)
         dc = left - c128
 
         def cut(s, _):
-            r0 = pl.multiple_of(s * STRIP, STRIP)
+            r0 = s * STRIP
             w = []
             for q in range(2):
                 block = ext[q, pl.ds(r8 + r0, STRIP + 8), pl.ds(c128, 3 * H)]
@@ -135,7 +127,9 @@
                 al[k // 2, rows, pl.ds((k % 2) * H, H)] = low
             return 0
 
-        lax.fori_loop(0, N // STRIP, cut, 0, unroll=8)
+        for s in range(N // STRIP):
+            cut(s, 0)
+        yield
 
         def right_apply(t):
             for k, out in ((0, ye), (1, yo)):
@@ -153,9 +147,10 @@
             al[k, rows, cols] = low
 
         right_apply(0)
+        yield
 
         def rows_forward(s, _):
-            r0 = pl.multiple_of(s * STRIP, STRIP)
+            r0 = s * STRIP
             up, down = pl.ds(r0, STRIP), pl.ds(r0 + H, STRIP)
             for k, src in ((0, ye), (1, yo)):
                 cols = pl.ds(k * H, H)
@@ -167,13 +162,15 @@
                     put(1, dest, cols, a - b)
             return 0
 
-        lax.fori_loop(0, H // STRIP, rows_forward, 0, unroll=4)
+        for s in range(H // STRIP):
+            rows_forward(s, 0)
+        yield
         left_apply(1)
-        fetch.wait()
-        amp[...] = mm(mm(sel_ref[0], raw[...]).astype(jnp.bfloat16), sel_ref[1])
+        amp[...] = mm(mm(sel_ref[0], amps_ref[j]).astype(jnp.bfloat16), sel_ref[1])
+        yield
 
         def modulus(s, _):
-            r0 = pl.multiple_of(s * STRIP, STRIP)
+            r0 = s * STRIP
             up, down = pl.ds(r0, STRIP), pl.ds(r0 + H, STRIP)
             for k, src in ((0, ye), (1, yo)):
                 re, im = src[up, :], src[down, :]
@@ -183,11 +180,14 @@
                 put(k, down, slice(None), im * f)
             return 0
 
-        lax.fori_loop(0, H // STRIP, modulus, 0, unroll=4)
+        for s in range(H // STRIP):
+            modulus(s, 0)
+        yield
         left_apply(0)
+        yield
 
         def rows_back(s, _):
-            r0 = pl.multiple_of(s * STRIP, STRIP)
+            r0 = s * STRIP
             up, down = pl.ds(r0, STRIP), pl.ds(r0 + H, STRIP)
             for q, src_rows in ((0, up), (1, down)):
                 part = pl.ds(q * H, H)
@@ -197,11 +197,14 @@
                     put(1, dest, part, z[:, H:])
             return 0
 
-        lax.fori_loop(0, H // STRIP, rows_back, 0, unroll=4)
+        for s in range(H // STRIP):
+            rows_back(s, 0)
+        yield
         right_apply(1)
+        yield
 
         def finish(s, _):
-            r0 = pl.multiple_of(s * STRIP, STRIP)
+            r0 = s * STRIP
             rows = pl.ds(r0, STRIP)
             e_re, e_im = ye[rows, :H], ye[rows, H:]
             o_re, o_im = yo[rows, :H], yo[rows, H:]
@@ -210,32 +213,60 @@
                 cols = pl.ds(k * H, H)
                 br = e_re + o_re if k == 0 else e_re - o_re
                 bi = e_im + o_im if k == 0 else e_im - o_im
-                cr = br - psi[0, rows, cols]
-                ci = bi - psi[1, rows, cols]
+                cr = (br - psi[0, rows, cols]) * valid
+                ci = (bi - psi[1, rows, cols]) * valid
                 pr, pi = probe_ref[0, k, rows, :], probe_ref[1, k, rows, :]
                 wr, wi = win[0, rows, cols], win[1, rows, cols]
                 term[0].append(pr * cr + pi * ci)
                 term[1].append(pr * ci - pi * cr)
                 part_ref[0, k, rows, :] += wr * cr + wi * ci
                 part_ref[1, k, rows, :] += wr * ci - wi * cr
-                part_ref[2, k, rows, :] += wr * wr + wi * wi
+                part_ref[2, k, rows, :] += (wr * wr + wi * wi) * valid
             for q in range(2):
                 deposit(sums_ref.at[q], r8 + r0, c128, dr, dc, lane, term[q])
             return 0
 
-        lax.fori_loop(0, N // STRIP, finish, 0, unroll=8)
-
-    def visit(i, _):
+        for s in range(N // STRIP):
+            finish(s, 0)
+        yield
+
+    def visit(i, found):
         j = band * 64 + i
-        y, x = pos_ref[2 * j], pos_ref[2 * j + 1]
-
-        @pl.when(x // N == my_col)
+        mine = pos_ref[2 * j + 1] // N == my_col
+
+        @pl.when(mine)
         def _():
-            process(i, y - band * N, x - my_col * N)
-
+            todo[found] = i
+
+        return found + mine.astype(jnp.int32)
+
+    count = lax.fori_loop(0, 64, visit, 0)
+
+    def pair(k, _):
+        lanes = []
+        for half in range(2):
+            at = 2 * k + half
+            i = todo[jnp.minimum(at, count - 1)]
+            j = band * 64 + i
+            valid = (at < count).astype(jnp.float32)
+            lanes.append(
+                process(
+                    work[7 * half : 7 * half + 7],
+                    i,
+                    pos_ref[2 * j] - band * N,
+                    pos_ref[2 * j + 1] - my_col * N,
+                    valid,
+                )
+            )
+        next(lanes[0])
+        alive = [True, True]
+        while any(alive):
+            for half in (1, 0):
+                if alive[half]:
+                    alive[half] = next(lanes[half], 0) is None
         return 0
 
-    lax.fori_loop(0, 64, visit, 0)
+    lax.fori_loop(0, (count + 1) // 2, pair, 0)
     if not first:
         return
 
@@ -285,20 +316,22 @@
             jax.ShapeDtypeStruct((3, 2, N, H), f32),
             jax.ShapeDtypeStruct((2 * NEAR,), jnp.int32),
         ),
-        in_specs=[SMEM, SMEM, VMEM, VMEM, ANY, VMEM, VMEM, VMEM],
+        in_specs=[SMEM, SMEM, VMEM, VMEM, VMEM, VMEM, VMEM, VMEM],
         out_specs=(VMEM, VMEM, SMEM),
         scratch_shapes=[
-            pltpu.VMEM((N, N), bf16),
-            pltpu.VMEM((N, N), f32),
-            pltpu.VMEM((2, N, N), f32),
-            pltpu.VMEM((2, N, N), f32),
-            pltpu.VMEM((2, N, N), bf16),
-            pltpu.VMEM((2, N, N), bf16),
-            pltpu.VMEM((N, N), f32),
-            pltpu.VMEM((N, N), f32),
-            pltpu.SemaphoreType.DMA,
+            pltpu.SMEM((64,), jnp.int32),
+            *2
+            * (
+                pltpu.VMEM((N, N), f32),
+                pltpu.VMEM((2, N, N), f32),
+                pltpu.VMEM((2, N, N), f32),
+                pltpu.VMEM((2, N, N), bf16),
+                pltpu.VMEM((2, N, N), bf16),
+                pltpu.VMEM((N, N), f32),
+                pltpu.VMEM((N, N), f32),
+            ),
         ],
-        compiler_params=pltpu.CompilerParams(vmem_limit_bytes=40 * 2**20),
+        compiler_params=pltpu.CompilerParams(vmem_limit_bytes=24 * 2**20),
         name="patterns",
     )(pos, place, ext, probe, gathered, high, low, sel)
 
@@ -358,32 +391,47 @@
 TOP, END = slice(0, N), slice(N, 2 * N)
 
 
+class Bulk:
+    def __init__(self, copies, src, dst, peer, k=None):
+        self.whole, self.k = copies.make(src, dst, peer, k)
+        self.copies, self.src, self.dst, self.peer = copies, src, dst, peer
+
+    def start(self, first=0, stop=4):
+        for part in range(first, stop):
+            rows = pl.ds(part * 64, 64)
+            self.copies.make(
+                self.src.at[:, rows], self.dst.at[:, rows], self.peer, self.k
+            )[0].start()
+
+
 class Halo:
     def __init__(self, copies, tile, ext, row, col, core):
         left, right, up, down = around(row, col)
         self.core = core
-        self.below, _ = copies.make(tile, ext.at[:, END, TOP], (up, col))
-        self.right, _ = copies.make(tile, ext.at[:, TOP, END], (row, left))
+        self.below = Bulk(copies, tile, ext.at[:, END, TOP], (up, col))
+        self.right = Bulk(copies, tile, ext.at[:, TOP, END], (row, left))
         corner = ext.at[:, END, END]
-        self.diag, k = copies.make(tile, corner, (up, left))
-        self.onward, _ = copies.make(ext.at[:, END, TOP], corner, (row, left), k)
-
-    def start_sides(self):
-        self.right.start()
+        self.diag = Bulk(copies, tile, corner, (up, left))
+        self.onward, _ = copies.make(
+            ext.at[:, END, TOP], corner, (row, left), self.diag.k
+        )
+
+    def start_sides(self, first=0, stop=4):
+        self.right.start(first, stop)
 
         @pl.when(self.core == 0)
         def _():
-            self.diag.start()
+            self.diag.start(first, stop)
 
     def finish(self):
-        self.below.wait_recv()
+        self.below.whole.wait_recv()
 
         @pl.when(self.core == 1)
         def _():
             self.onward.start()
 
-        self.below.wait_send()
-        self.right.wait()
+        self.below.whole.wait_send()
+        self.right.whole.wait()
         self.onward.wait()
 
 
@@ -419,8 +467,6 @@
     to_ahead = copies.send(amps_ref, mine, ahead)
     to_behind = copies.send(amps_ref, mine, behind)
     halo = Halo(copies, obj_ref, ext_ref, row, col, core)
-    halo.below.start()
-    halo.start_sides()
     own = [
         pltpu.make_async_copy(amps_ref, mine, own_sem.at[0]),
         pltpu.make_async_copy(obj_ref, ext_ref.at[:, TOP, TOP], own_sem.at[1]),
@@ -431,6 +477,8 @@
     to_beside.wait_recv()
     ahead_2 = copies.send(other, other, ahead)
     behind_2 = copies.send(other, other, behind)
+    halo.below.start()
+    halo.start_sides()
     rest.append(copies.send(other, other, twin))
     far = []
     for low, high, side in ((to_ahead, to_behind, ylo), (ahead_2, behind_2, 1 - ylo)):
@@ -546,20 +594,35 @@
             weights[...] += mm(to_row, a) + mm(to_row, b)
             return 0
 
-        lax.fori_loop(start, stop, add, 0)
+        lax.fori_loop(start, stop, add, 0, unroll=4)
 
     on_pair = copies.send(part_ref.at[:, 1 - core], pair, twin)
     edge = sums_ref.at[:, END, END]
     inside, k = copies.make(edge, corner, twin)
-    outside, _ = copies.make(edge, corner, (down, right), k)
-    down_sums, k = copies.make(sums_ref.at[:, END, TOP], from_above, (down, col))
-    down_joint, _ = copies.make(low, from_above, (down, col), k)
-    to_right, _ = copies.make(sums_ref.at[:, TOP, END], from_left, (row, right))
+    outside = Bulk(copies, edge, corner, (down, right), k)
+    down_sums = Bulk(copies, sums_ref.at[:, END, TOP], from_above, (down, col))
+    down_joint = Bulk(copies, low, from_above, (down, col), down_sums.k)
+    to_right = Bulk(copies, sums_ref.at[:, TOP, END], from_left, (row, right))
+
+    def send_down(first, stop):
+        @pl.when(core == 0)
+        def _():
+            down_sums.start(first, stop)
+
+        @pl.when(core == 1)
+        def _():
+            down_joint.start(first, stop)
+
+    def send_right(first, stop):
+        @pl.when(core == 1)
+        def _():
+            outside.start(first, stop)
+
+        to_right.start(first, stop)
 
     @pl.when(core == 0)
     def _():
         inside.start()
-        down_sums.start()
 
     weights[...] = jnp.zeros((N, N), jnp.float32)
     for k in range(2):
@@ -582,8 +645,8 @@
     def _():
         inside.wait_recv()
         low[...] = sums_ref[:, END, TOP] + corner[...]
-        down_joint.start()
-
+
+    send_down(0, 2)
     add_weights(0, 16)
     finish(group)
     mine = pl.ds(pl.multiple_of(x * 64, 64), 64)
@@ -597,28 +660,26 @@
         for d in (1, 2, 3)
     ]
 
-    @pl.when(core == 1)
-    def _():
-        outside.start()
-
-    to_right.start()
+    send_right(0, 2)
     add_weights(16, 24)
     finish(group)
     mine = pl.ds(pl.multiple_of(z * 16, 16), 16)
     small[...] = (quarter[:, mine, :] + from_z[0]) + (from_z[1] + from_z[2])
     group = [copies.send(small, from_y.at[y], peer) for peer in on_y]
     from_y[y] = small[...]
+    send_down(2, 3 if last else 4)
+    send_right(2, 3 if last else 4)
     add_weights(24, 32)
 
     def object_update():
-        to_right.wait()
-        down_sums.wait()
+        to_right.whole.wait()
+        down_sums.whole.wait()
 
         @pl.when(core == 0)
         def _():
-            outside.wait_recv()
-
-        outside.wait_send()
+            outside.whole.wait_recv()
+
+        outside.whole.wait_send()
         for r in range(0, N, STRIP):
             rows = pl.ds(r, STRIP)
             scale = 1.0 / (weights[rows, :] + object_regular)
@@ -628,10 +689,6 @@
                 total = total + jnp.where(core == 0, corner[q, rows, :], 0.0)
                 tile_ref[q, rows, TOP] = ext_ref[q, rows, TOP] + total * scale
 
-    if not last:
-        object_update()
-        halo = Halo(copies, tile_ref.at[:, TOP, TOP], tile_ref, row, col, core)
-        halo.below.start()
     finish(group)
     total = (from_y[0] + from_y[1]) + (from_y[2] + from_y[3])
     rows = pl.ds(pl.multiple_of(x * 64 + z * 16, 16), 16)
@@ -640,17 +697,25 @@
             total[2] + probe_regular
         )
     piece = out_ref.at[:, core, rows, :]
-    finish([copies.send(piece, piece, peer) for peer in on_z])
+    group = [copies.send(piece, piece, peer) for peer in on_z]
+    if last:
+        send_down(3, 4)
+        send_right(3, 4)
+    else:
+        object_update()
+        halo = Halo(copies, tile_ref.at[:, TOP, TOP], tile_ref, row, col, core)
+        halo.below.start()
+    finish(group)
     piece = out_ref.at[:, core, pl.ds(pl.multiple_of(x * 64, 64), 64), :]
     group = [copies.send(piece, piece, peer) for peer in on_x]
-    if last:
-        object_update()
-    else:
+    if not last:
         halo.start_sides()
     finish(group)
     piece = out_ref.at[:, core]
     to_twin = copies.send(piece, piece, twin)
-    if not last:
+    if last:
+        object_update()
+    else:
         halo.finish()
     to_twin.wait()
 
@@ -688,7 +753,7 @@
         compiler_params=pltpu.CompilerParams(
             collective_id=3 if last else 2,
             has_side_effects=True,
-            vmem_limit_bytes=32 * 2**20,
+            vmem_limit_bytes=14 * 2**20,
         ),
         name="finish" if last else "exchange",
     )(sums, near, ext, partials, probe)

time: 216 us -> 190 us (0.88)
  Pallas kernels: 208 us -> 185 us
  local copies, waits for them, and re-layouts: 6.27 us -> 3.06 us
    pallas_call x2, Pallas kernels: 121 us -> 106 us  [run_exchange(): pl.pallas_call(functools.partial(exchange_kernel, last), out_shape=(jax.S...]
    pallas_call x2, Pallas kernels: 27.4 us -> 19.5 us  [run_patterns(): pl.pallas_call(functools.partial(pattern_kernel, first), out_shape=(jax.S...]
    unnamed x14 -> x12, local copies, waits for them, and re-layouts: 5 us -> 1.79 us
where the time goes in v4:
time: 190 us
  Pallas kernels  185 us (97%)
  local copies, waits for them, and re-layouts  3.06 us (2%)
    pallas_call x2, Pallas kernels, run_exchange(): pl.pallas_call(functools.partial(exchange_kernel, last), out_shape=(jax.S...  106 us
    pallas_call x1, Pallas kernels, run_start(): pl.pallas_call(start_kernel, out_shape=(jax.ShapeDtypeStruct((2, 2 * N, 2...  59.9 us
    pallas_call x2, Pallas kernels, run_patterns(): pl.pallas_call(functools.partial(pattern_kernel, first), out_shape=(jax.S...  19.5 us

profile of v4, /device:TPU:1, one launch (start us, length us, event | category | flops | bytes accessed | tf_op | source)
XLA Modules:
  0.0 189.9 jit_solution(5743405680184605939)
XLA Ops:
  0.6 0.0 copy-start.2
  0.6 0.0 copy-start
  0.7 0.0 copy-start.1
  0.7 0.0 copy-start.4
  0.7 0.0 copy-start.3
  0.7 0.1 pad_add_fusion.place_ref
  0.8 1.0 copy.9
  1.7 0.2 reshape.7.pos_ref
  1.9 1.1 slice_bitcast_fusion.3
  3.0 0.0 copy-done.4
  3.0 0.0 copy-done.3
  3.0 59.9 %start.1 = (f32[2,512,512]{2,1,0:T(8,128)S(1)}, bf16[64,256,256]{2,1,0:T(8,128)(2,1)S(1)}) custom-call(f32[2,256,256]{2,1,0:T(8,128)S(1)} %copy-done.3, bf16[4,256,256]{2,1,0:T(8,128)(2,1)S(1)} %copy-done.4), custom_call_target="tpu_custom_call" | custom-call | tf_op jit(solution)/shard_map/start/pallas_call | solution.py:511
  63.0 0.0 copy-done.2
  63.0 0.0 copy-done
  63.0 0.0 copy-done.1
  63.0 10.1 %patterns.2 = (f32[2,512,512]{2,1,0:T(8,128)S(1)}, f32[3,2,256,128]{3,2,1,0:T(8,128)S(1)}, s32[64]{0:T(128)S(1)}) custom-call(s32[1024]{0:T(1024)S(1)} %reshape.7.pos_ref, s32[2]{0:T(128)S(1)} %pad_add_fusion.place_ref, f32[2,512,512]{2,1,0:T(8,128)S(1)} %get-tuple-element.13.ext.ext_ref, f32[2,2,256,128]{3,2,1,0:T(8,128)S(1)} %pad_maximum_fusion.probe_ref.old_ref, ...), custom_call_target="tpu_custom_call" | custom-call | tf_op jit(solution)/shard_map/patterns/pallas_call | solution.py:312
  73.1 58.8 %exchange.1 = (f32[2,512,512]{2,1,0:T(8,128)S(1)}, f32[2,2,256,128]{3,2,1,0:T(8,128)S(1)}) custom-call(f32[2,512,512]{2,1,0:T(8,128)S(1)} %get-tuple-element.15.sums_ref, s32[64]{0:T(128)S(1)} %get-tuple-element.16.near_ref, f32[2,512,512]{2,1,0:T(8,128)S(1)} %get-tuple-element.13.ext.ext_ref, f32[3,2,256,128]{3,2,1,0:T(8,128)S(1)} %get-tuple-element.17.part_ref, ...), custom_call_target="tpu_custom_call" | custom-call | tf_op jit(solution)/shard_map/exchange/pallas_call | solution.py:727
  131.9 9.4 %patterns.3 = (f32[2,512,512]{2,1,0:T(8,128)S(1)}, f32[3,2,256,128]{3,2,1,0:T(8,128)S(1)}, s32[64]{0:T(128)}) custom-call(s32[1024]{0:T(1024)S(1)} %reshape.7.pos_ref, s32[2]{0:T(128)S(1)} %pad_add_fusion.place_ref, f32[2,512,512]{2,1,0:T(8,128)S(1)} %get-tuple-element.18.ext.ext_ref, f32[2,2,256,128]{3,2,1,0:T(8,128)S(1)} %get-tuple-element.19.probe_ref.old_ref, ...), custom_call_target="tpu_custom_call" | custom-call | tf_op jit(solution)/shard_map/patterns/pallas_call | solution.py:312
  141.3 46.9 %finish.1 = (f32[2,256,256]{2,1,0:T(8,128)S(1)}, f32[2,2,256,128]{3,2,1,0:T(8,128)S(1)}) custom-call(f32[2,512,512]{2,1,0:T(8,128)S(1)} %get-tuple-element.20.sums_ref, s32[64]{0:T(128)S(1)} %get-tuple-element.16.near_ref, f32[2,512,512]{2,1,0:T(8,128)S(1)} %get-tuple-element.18.ext.ext_ref, f32[3,2,256,128]{3,2,1,0:T(8,128)S(1)} %get-tuple-element.21.part_ref, ...), custom_call_target="tpu_custom_call" | custom-call | tf_op jit(solution)/shard_map/finish/pallas_call | solution.py:727
  188.3 0.8 pad_maximum_fusion.1
  189.1 0.8 copy.14
  (3 shorter events, 0.1 us)
Async XLA Ops:
  0.6 62.3 %copy-start.2 = (bf16[2,256,256]{2,1,0:T(8,128)(2,1)S(1)}, bf16[2,256,256]{2,1,0:T(8,128)(2,1)}, u32[]{:S(2)}) copy-start(bf16[2,256,256]{2,1,0:T(8,128)(2,1)} %constant.20.sel_ref) | copy-start | bytes 786436
  0.6 62.3 %copy-start = (bf16[4,256,256]{2,1,0:T(8,128)(2,1)S(1)}, bf16[4,256,256]{2,1,0:T(8,128)(2,1)}, u32[]{:S(2)}) copy-start(bf16[4,256,256]{2,1,0:T(8,128)(2,1)} %constant.19.tl_ref) | copy-start | bytes 1572868
  0.7 62.3 %copy-start.1 = (bf16[4,256,256]{2,1,0:T(8,128)(2,1)S(1)}, bf16[4,256,256]{2,1,0:T(8,128)(2,1)}, u32[]{:S(2)}) copy-start(bf16[4,256,256]{2,1,0:T(8,128)(2,1)} %constant.16.th_ref) | copy-start | bytes 1572868
  0.7 2.4 %copy-start.4 = (bf16[4,256,256]{2,1,0:T(8,128)(2,1)S(1)}, bf16[4,256,256]{2,1,0:T(8,128)(2,1)}, u32[]{:S(2)}) copy-start(bf16[4,256,256]{2,1,0:T(8,128)(2,1)} %amps_ref.1) | copy-start | bytes 1572868
  0.7 2.4 %copy-start.3 = (f32[2,256,256]{2,1,0:T(8,128)S(1)}, f32[2,256,256]{2,1,0:T(8,128)}, u32[]{:S(2)}) copy-start(f32[2,256,256]{2,1,0:T(8,128)} %obj_ref.1) | copy-start | bytes 1572868

commit v5 on v4

--- a/solution.py
+++ b/solution.py
@@ -441,6 +441,7 @@
     twin = device(z, y, x, 1 - core)
     beside = device(z, y + 1 - 2 * (y % 2), x, core)
     ahead, behind = device(z, y, (x + 1) % 4, core), device(z, y, (x + 3) % 4, core)
+    freer = device(z, y, (x + 1 + 2 * (y % 2)) % 4, core)
     greet(
         [
             twin,
@@ -488,8 +489,10 @@
         whole = block(x + 3, side)
         rest.append(copies.send(whole, whole, twin))
         high.wait_recv()
-        part = block(x + 1, side, 2, 2)
-        far.append((copies.send(part, part, behind), block(x + 2, side, 2, 2)))
+        part = block(x + 1, side, 3, 1)
+        far.append((copies.send(part, part, behind), block(x + 2, side, 3, 1)))
+        part = block(x + 3 - 2 * ylo, side, 2, 1)
+        far.append((copies.send(part, part, freer), block(x + 2, side, 2, 1)))
         whole = block(x + 1, side)
         rest.append(copies.send(whole, whole, twin))
     for copy, part in far:
@@ -507,7 +510,7 @@
 
 
 def run_start(obj, amplitudes):
-    count = 3 + 3 + 1 + 3 + 8 + 4
+    count = 3 + 2 + 3 + 12 + 6
     return pl.pallas_call(
         start_kernel,
         out_shape=(
@@ -667,8 +670,8 @@
     small[...] = (quarter[:, mine, :] + from_z[0]) + (from_z[1] + from_z[2])
     group = [copies.send(small, from_y.at[y], peer) for peer in on_y]
     from_y[y] = small[...]
-    send_down(2, 3 if last else 4)
-    send_right(2, 3 if last else 4)
+    send_down(2, 4)
+    send_right(2, 4)
     add_weights(24, 32)
 
     def object_update():
@@ -698,19 +701,16 @@
         )
     piece = out_ref.at[:, core, rows, :]
     group = [copies.send(piece, piece, peer) for peer in on_z]
-    if last:
-        send_down(3, 4)
-        send_right(3, 4)
-    else:
+    if not last:
         object_update()
         halo = Halo(copies, tile_ref.at[:, TOP, TOP], tile_ref, row, col, core)
         halo.below.start()
     finish(group)
     piece = out_ref.at[:, core, pl.ds(pl.multiple_of(x * 64, 64), 64), :]
     group = [copies.send(piece, piece, peer) for peer in on_x]
+    finish(group)
     if not last:
         halo.start_sides()
-    finish(group)
     piece = out_ref.at[:, core]
     to_twin = copies.send(piece, piece, twin)
     if last:

time: 190 us -> 181 us (0.953)
  Pallas kernels: 185 us -> 176 us
    pallas_call x2, Pallas kernels: 106 us -> 101 us  [run_exchange(): pl.pallas_call(functools.partial(exchange_kernel, last), out_shape=(jax.S...]
    pallas_call x1, Pallas kernels: 59.9 us -> 55.5 us  [run_start(): pl.pallas_call(start_kernel, out_shape=(jax.ShapeDtypeStruct((2, 2 * N, 2...]
where the time goes in v5:
time: 181 us; the launch traced here: 180 us
  Pallas kernels  176 us (97%)
  local copies, waits for them, and re-layouts  3.06 us (2%)
    pallas_call x2, Pallas kernels, run_exchange(): pl.pallas_call(functools.partial(exchange_kernel, last), out_shape=(jax.S...  101 us
    pallas_call x1, Pallas kernels, run_start(): pl.pallas_call(start_kernel, out_shape=(jax.ShapeDtypeStruct((2, 2 * N, 2...  55.5 us
    pallas_call x2, Pallas kernels, run_patterns(): pl.pallas_call(functools.partial(pattern_kernel, first), out_shape=(jax.S...  19.5 us

profile of v5, /device:TPU:1, one launch (start us, length us, event | category | flops | bytes accessed | tf_op | source)
XLA Modules:
  0.0 180.3 jit_solution(6602225170957020184)
XLA Ops:
  0.6 0.0 copy-start.2
  0.6 0.0 copy-start
  0.7 0.0 copy-start.1
  0.7 0.0 copy-start.4
  0.7 0.0 copy-start.3
  0.7 0.1 pad_add_fusion.place_ref
  0.8 1.0 copy.9
  1.7 0.2 reshape.7.pos_ref
  1.9 1.1 slice_bitcast_fusion.3
  3.0 0.0 copy-done.4
  3.0 0.0 copy-done.3
  3.0 55.5 %start.1 = (f32[2,512,512]{2,1,0:T(8,128)S(1)}, bf16[64,256,256]{2,1,0:T(8,128)(2,1)S(1)}) custom-call(f32[2,256,256]{2,1,0:T(8,128)S(1)} %copy-done.3, bf16[4,256,256]{2,1,0:T(8,128)(2,1)S(1)} %copy-done.4), custom_call_target="tpu_custom_call" | custom-call | tf_op jit(solution)/shard_map/start/pallas_call | solution.py:514
  58.5 0.0 copy-done.2
  58.5 0.0 copy-done
  58.5 0.0 copy-done.1
  58.5 10.1 %patterns.2 = (f32[2,512,512]{2,1,0:T(8,128)S(1)}, f32[3,2,256,128]{3,2,1,0:T(8,128)S(1)}, s32[64]{0:T(128)S(1)}) custom-call(s32[1024]{0:T(1024)S(1)} %reshape.7.pos_ref, s32[2]{0:T(128)S(1)} %pad_add_fusion.place_ref, f32[2,512,512]{2,1,0:T(8,128)S(1)} %get-tuple-element.13.ext.ext_ref, f32[2,2,256,128]{3,2,1,0:T(8,128)S(1)} %pad_maximum_fusion.probe_ref.old_ref, ...), custom_call_target="tpu_custom_call" | custom-call | tf_op jit(solution)/shard_map/patterns/pallas_call | solution.py:312
  68.6 58.6 %exchange.1 = (f32[2,512,512]{2,1,0:T(8,128)S(1)}, f32[2,2,256,128]{3,2,1,0:T(8,128)S(1)}) custom-call(f32[2,512,512]{2,1,0:T(8,128)S(1)} %get-tuple-element.15.sums_ref, s32[64]{0:T(128)S(1)} %get-tuple-element.16.near_ref, f32[2,512,512]{2,1,0:T(8,128)S(1)} %get-tuple-element.13.ext.ext_ref, f32[3,2,256,128]{3,2,1,0:T(8,128)S(1)} %get-tuple-element.17.part_ref, ...), custom_call_target="tpu_custom_call" | custom-call | tf_op jit(solution)/shard_map/exchange/pallas_call | solution.py:727
  127.3 9.4 %patterns.3 = (f32[2,512,512]{2,1,0:T(8,128)S(1)}, f32[3,2,256,128]{3,2,1,0:T(8,128)S(1)}, s32[64]{0:T(128)}) custom-call(s32[1024]{0:T(1024)S(1)} %reshape.7.pos_ref, s32[2]{0:T(128)S(1)} %pad_add_fusion.place_ref, f32[2,512,512]{2,1,0:T(8,128)S(1)} %get-tuple-element.18.ext.ext_ref, f32[2,2,256,128]{3,2,1,0:T(8,128)S(1)} %get-tuple-element.19.probe_ref.old_ref, ...), custom_call_target="tpu_custom_call" | custom-call | tf_op jit(solution)/shard_map/patterns/pallas_call | solution.py:312
  136.6 42.0 %finish.1 = (f32[2,256,256]{2,1,0:T(8,128)S(1)}, f32[2,2,256,128]{3,2,1,0:T(8,128)S(1)}) custom-call(f32[2,512,512]{2,1,0:T(8,128)S(1)} %get-tuple-element.20.sums_ref, s32[64]{0:T(128)S(1)} %get-tuple-element.16.near_ref, f32[2,512,512]{2,1,0:T(8,128)S(1)} %get-tuple-element.18.ext.ext_ref, f32[3,2,256,128]{3,2,1,0:T(8,128)S(1)} %get-tuple-element.21.part_ref, ...), custom_call_target="tpu_custom_call" | custom-call | tf_op jit(solution)/shard_map/finish/pallas_call | solution.py:727
  178.7 0.8 pad_maximum_fusion.1
  179.5 0.8 copy.14
  (3 shorter events, 0.1 us)
Async XLA Ops:
  0.6 57.9 %copy-start.2 = (bf16[2,256,256]{2,1,0:T(8,128)(2,1)S(1)}, bf16[2,256,256]{2,1,0:T(8,128)(2,1)}, u32[]{:S(2)}) copy-start(bf16[2,256,256]{2,1,0:T(8,128)(2,1)} %constant.20.sel_ref) | copy-start | bytes 786436
  0.6 57.9 %copy-start = (bf16[4,256,256]{2,1,0:T(8,128)(2,1)S(1)}, bf16[4,256,256]{2,1,0:T(8,128)(2,1)}, u32[]{:S(2)}) copy-start(bf16[4,256,256]{2,1,0:T(8,128)(2,1)} %constant.19.tl_ref) | copy-start | bytes 1572868
  0.7 57.9 %copy-start.1 = (bf16[4,256,256]{2,1,0:T(8,128)(2,1)S(1)}, bf16[4,256,256]{2,1,0:T(8,128)(2,1)}, u32[]{:S(2)}) copy-start(bf16[4,256,256]{2,1,0:T(8,128)(2,1)} %constant.16.th_ref) | copy-start | bytes 1572868
  0.7 2.4 %copy-start.4 = (bf16[4,256,256]{2,1,0:T(8,128)(2,1)S(1)}, bf16[4,256,256]{2,1,0:T(8,128)(2,1)}, u32[]{:S(2)}) copy-start(bf16[4,256,256]{2,1,0:T(8,128)(2,1)} %amps_ref.1) | copy-start | bytes 1572868
  0.7 2.4 %copy-start.3 = (f32[2,256,256]{2,1,0:T(8,128)S(1)}, f32[2,256,256]{2,1,0:T(8,128)}, u32[]{:S(2)}) copy-start(f32[2,256,256]{2,1,0:T(8,128)} %obj_ref.1) | copy-start | bytes 1572868

commit v6 on v5

--- a/solution.py
+++ b/solution.py
@@ -704,10 +704,12 @@
     if not last:
         object_update()
         halo = Halo(copies, tile_ref.at[:, TOP, TOP], tile_ref, row, col, core)
-        halo.below.start()
+        halo.below.start(0, 2)
     finish(group)
     piece = out_ref.at[:, core, pl.ds(pl.multiple_of(x * 64, 64), 64), :]
     group = [copies.send(piece, piece, peer) for peer in on_x]
+    if not last:
+        halo.below.start(2, 4)
     finish(group)
     if not last:
         halo.start_sides()

time: 181 us -> 190 us (1.050); the launches traced: 180 us -> 186 us
  Pallas kernels: 176 us -> 182 us
    pallas_call x2, Pallas kernels: 101 us -> 107 us  [run_exchange(): pl.pallas_call(functools.partial(exchange_kernel, last), out_shape=(jax.S...]
where the time goes in v6:
time: 190 us; the launch traced here: 186 us
  Pallas kernels  182 us (96%)
  local copies, waits for them, and re-layouts  3.06 us (2%)
    pallas_call x2, Pallas kernels, run_exchange(): pl.pallas_call(functools.partial(exchange_kernel, last), out_shape=(jax.S...  107 us
    pallas_call x1, Pallas kernels, run_start(): pl.pallas_call(start_kernel, out_shape=(jax.ShapeDtypeStruct((2, 2 * N, 2...  55.5 us
    pallas_call x2, Pallas kernels, run_patterns(): pl.pallas_call(functools.partial(pattern_kernel, first), out_shape=(jax.S...  19.5 us

profile of v6, /device:TPU:1, one launch (start us, length us, event | category | flops | bytes accessed | tf_op | source)
XLA Modules:
  0.0 186.4 jit_solution(6692575426023184928)
XLA Ops:
  0.6 0.0 copy-start.2
  0.6 0.0 copy-start
  0.7 0.0 copy-start.1
  0.7 0.0 copy-start.4
  0.7 0.0 copy-start.3
  0.7 0.1 pad_add_fusion.place_ref
  0.8 1.0 copy.9
  1.7 0.2 reshape.7.pos_ref
  1.9 1.1 slice_bitcast_fusion.3
  3.0 0.0 copy-done.4
  3.0 0.0 copy-done.3
  3.0 55.5 %start.1 = (f32[2,512,512]{2,1,0:T(8,128)S(1)}, bf16[64,256,256]{2,1,0:T(8,128)(2,1)S(1)}) custom-call(f32[2,256,256]{2,1,0:T(8,128)S(1)} %copy-done.3, bf16[4,256,256]{2,1,0:T(8,128)(2,1)S(1)} %copy-done.4), custom_call_target="tpu_custom_call" | custom-call | tf_op jit(solution)/shard_map/start/pallas_call | solution.py:514
  58.5 0.0 copy-done.2
  58.5 0.0 copy-done
  58.5 0.0 copy-done.1
  58.5 10.2 %patterns.2 = (f32[2,512,512]{2,1,0:T(8,128)S(1)}, f32[3,2,256,128]{3,2,1,0:T(8,128)S(1)}, s32[64]{0:T(128)S(1)}) custom-call(s32[1024]{0:T(1024)S(1)} %reshape.7.pos_ref, s32[2]{0:T(128)S(1)} %pad_add_fusion.place_ref, f32[2,512,512]{2,1,0:T(8,128)S(1)} %get-tuple-element.13.ext.ext_ref, f32[2,2,256,128]{3,2,1,0:T(8,128)S(1)} %pad_maximum_fusion.probe_ref.old_ref, ...), custom_call_target="tpu_custom_call" | custom-call | tf_op jit(solution)/shard_map/patterns/pallas_call | solution.py:312
  68.7 58.2 %exchange.1 = (f32[2,512,512]{2,1,0:T(8,128)S(1)}, f32[2,2,256,128]{3,2,1,0:T(8,128)S(1)}) custom-call(f32[2,512,512]{2,1,0:T(8,128)S(1)} %get-tuple-element.15.sums_ref, s32[64]{0:T(128)S(1)} %get-tuple-element.16.near_ref, f32[2,512,512]{2,1,0:T(8,128)S(1)} %get-tuple-element.13.ext.ext_ref, f32[3,2,256,128]{3,2,1,0:T(8,128)S(1)} %get-tuple-element.17.part_ref, ...), custom_call_target="tpu_custom_call" | custom-call | tf_op jit(solution)/shard_map/exchange/pallas_call | solution.py:729
  127.0 9.4 %patterns.3 = (f32[2,512,512]{2,1,0:T(8,128)S(1)}, f32[3,2,256,128]{3,2,1,0:T(8,128)S(1)}, s32[64]{0:T(128)}) custom-call(s32[1024]{0:T(1024)S(1)} %reshape.7.pos_ref, s32[2]{0:T(128)S(1)} %pad_add_fusion.place_ref, f32[2,512,512]{2,1,0:T(8,128)S(1)} %get-tuple-element.18.ext.ext_ref, f32[2,2,256,128]{3,2,1,0:T(8,128)S(1)} %get-tuple-element.19.probe_ref.old_ref, ...), custom_call_target="tpu_custom_call" | custom-call | tf_op jit(solution)/shard_map/patterns/pallas_call | solution.py:312
  136.3 48.4 %finish.1 = (f32[2,256,256]{2,1,0:T(8,128)S(1)}, f32[2,2,256,128]{3,2,1,0:T(8,128)S(1)}) custom-call(f32[2,512,512]{2,1,0:T(8,128)S(1)} %get-tuple-element.20.sums_ref, s32[64]{0:T(128)S(1)} %get-tuple-element.16.near_ref, f32[2,512,512]{2,1,0:T(8,128)S(1)} %get-tuple-element.18.ext.ext_ref, f32[3,2,256,128]{3,2,1,0:T(8,128)S(1)} %get-tuple-element.21.part_ref, ...), custom_call_target="tpu_custom_call" | custom-call | tf_op jit(solution)/shard_map/finish/pallas_call | solution.py:729
  184.8 0.8 pad_maximum_fusion.1
  185.6 0.8 copy.14
  (3 shorter events, 0.1 us)
Async XLA Ops:
  0.6 57.9 %copy-start.2 = (bf16[2,256,256]{2,1,0:T(8,128)(2,1)S(1)}, bf16[2,256,256]{2,1,0:T(8,128)(2,1)}, u32[]{:S(2)}) copy-start(bf16[2,256,256]{2,1,0:T(8,128)(2,1)} %constant.20.sel_ref) | copy-start | bytes 786436
  0.6 57.9 %copy-start = (bf16[4,256,256]{2,1,0:T(8,128)(2,1)S(1)}, bf16[4,256,256]{2,1,0:T(8,128)(2,1)}, u32[]{:S(2)}) copy-start(bf16[4,256,256]{2,1,0:T(8,128)(2,1)} %constant.19.tl_ref) | copy-start | bytes 1572868
  0.7 57.9 %copy-start.1 = (bf16[4,256,256]{2,1,0:T(8,128)(2,1)S(1)}, bf16[4,256,256]{2,1,0:T(8,128)(2,1)}, u32[]{:S(2)}) copy-start(bf16[4,256,256]{2,1,0:T(8,128)(2,1)} %constant.16.th_ref) | copy-start | bytes 1572868
  0.7 2.4 %copy-start.4 = (bf16[4,256,256]{2,1,0:T(8,128)(2,1)S(1)}, bf16[4,256,256]{2,1,0:T(8,128)(2,1)}, u32[]{:S(2)}) copy-start(bf16[4,256,256]{2,1,0:T(8,128)(2,1)} %amps_ref.1) | copy-start | bytes 1572868
  0.7 2.4 %copy-start.3 = (f32[2,256,256]{2,1,0:T(8,128)S(1)}, f32[2,256,256]{2,1,0:T(8,128)}, u32[]{:S(2)}) copy-start(f32[2,256,256]{2,1,0:T(8,128)} %obj_ref.1) | copy-start | bytes 1572868
